TPU v7x, 256 devices: a whole 4x4x8 slice. The times are simulated.
256 devices in a mesh: pair: 4 (over z_hi), row: 8 (over z_lo, y), col: 8 (over x, core).
Axes of the slice: x: 4, y: 4, z: 8 (z_hi: 4, z_lo: 2; z = z_hi * 2 + z_lo), core: 2. Of those that a mesh axis runs over, the one named last changes fastest.
Arguments:
- conductance: float32 [2048, 4096], P('row', 'col'), may hold values from 0.25 to 4
- valid_mask: int32 [2048, 4096], P('row', 'col'), may hold values 0 or 1
- focal_cells: int32 [8, 2], P('pair'), may hold values from 0 to 8388607
- initial_volts: float32 [8, 2048, 4096], P('pair', 'row', 'col'), may hold values from -2 to 2
Outputs:
- voltages: float32 [8, 2048, 4096], P('pair', 'row', 'col')
- current_sum: float32 [2048, 4096], P('row', 'col')
- current_max: float32 [2048, 4096], P('row', 'col')
All inputs are finite; a program needn't handle non-finite values. No bound on the sum of `valid_mask` on one device may be relied on, other than what follows from the above.
Results may differ from a plain program's by a relative error of at most 0.0039.
Values sent between devices are 32-bit elements; how exact they have to be, the bound alone decides.
A program may use at most 64 MiB of HBM per device.

v0:
```python
import jax
import jax.numpy as jnp
from jax import lax
from jax.sharding import PartitionSpec as P

ITERS = 6


LEAKAGE = 0.01


def padded_2(block, sides, width):
    for axis, dim in sides:
        count = lax.axis_size(axis)
        forward = [(i, i + 1) for i in range(count - 1)]
        backward = [(target, source) for source, target in forward]
        low = lax.ppermute(
            lax.slice_in_dim(block, block.shape[dim] - width, None, axis=dim), axis, forward
        )
        high = lax.ppermute(lax.slice_in_dim(block, 0, width, axis=dim), axis, backward)
        block = jnp.concatenate([low, block, high], axis=dim)
    return block


def link_set(padded_cond, padded_valid):
    centre_cond = padded_cond[1:-1, 1:-1]
    centre_valid = padded_valid[1:-1, 1:-1]

    def link_value(other_cond, other_valid):
        return 0.5 * (centre_cond + other_cond) * centre_valid * other_valid

    north = link_value(padded_cond[:-2, 1:-1], padded_valid[:-2, 1:-1])
    south = link_value(padded_cond[2:, 1:-1], padded_valid[2:, 1:-1])
    west = link_value(padded_cond[1:-1, :-2], padded_valid[1:-1, :-2])
    east = link_value(padded_cond[1:-1, 2:], padded_valid[1:-1, 2:])
    diagonal = north + south + west + east + LEAKAGE * centre_cond + (1.0 - centre_valid)
    inverse = 1.0 / jnp.maximum(diagonal, 1.0)
    return ((north, south, west, east, diagonal), inverse)


def apply_padded(field, wide, links):
    north, south, west, east, diagonal = links
    beside = north * wide[..., :-2, 1:-1] + south * wide[..., 2:, 1:-1]
    beside = beside + west * wide[..., 1:-1, :-2] + east * wide[..., 1:-1, 2:]
    return diagonal * field - beside


def cell_current(field, wide, links):
    north, south, west, east, diagonal = links
    flows = jnp.abs(north * (field - wide[..., :-2, 1:-1])) + jnp.abs(
        south * (field - wide[..., 2:, 1:-1])
    )
    flows = (
        flows
        + jnp.abs(west * (field - wide[..., 1:-1, :-2]))
        + jnp.abs(east * (field - wide[..., 1:-1, 2:]))
    )
    return 0.5 * flows


def widen(field):
    return padded_2(field, (("row", 1), ("col", 2)), 1)


def apply_operator(field, links):
    return apply_padded(field, widen(field), links)


def squared_progress(residual, scaled):
    return lax.psum(jnp.sum(residual * scaled, axis=(1, 2)), ("row", "col"))


def on_device(conductance, valid_mask, focal_cells, initial_volts):
    tile_rows = conductance.shape[0]
    tile_cols = conductance.shape[1]
    valid = valid_mask.astype(jnp.float32)
    cond = conductance * valid
    padded = padded_2(jnp.stack([cond, valid]), (("row", 1), ("col", 2)), 1)
    links, inverse = link_set(padded[0], padded[1])
    row_start = lax.axis_index("row") * tile_rows
    col_start = lax.axis_index("col") * tile_cols
    width_all = tile_cols * lax.axis_size("col")
    row_ids = row_start + jnp.arange(tile_rows, dtype=jnp.int32)
    col_ids = col_start + jnp.arange(tile_cols, dtype=jnp.int32)
    flat_index = row_ids[:, None] * width_all + col_ids[None, :]
    sources = focal_cells[:, 0][:, None, None]
    grounds = focal_cells[:, 1][:, None, None]
    inject = (flat_index[None] == sources).astype(jnp.float32) - (
        flat_index[None] == grounds
    ).astype(jnp.float32)
    voltage = initial_volts
    residual = inject - apply_operator(voltage, links)
    scaled = inverse * residual
    search = scaled
    progress = squared_progress(residual, scaled)
    for iteration in range(ITERS):
        image = apply_operator(search, links)
        curve = lax.psum(jnp.sum(search * image, axis=(1, 2)), ("row", "col"))
        step_size = (progress / curve)[:, None, None]
        voltage = voltage + step_size * search
        residual = residual - step_size * image
        scaled = inverse * residual
        renewed = squared_progress(residual, scaled)
        search = scaled + (renewed / progress)[:, None, None] * search
        progress = renewed
    current = cell_current(voltage, widen(voltage), links)
    local_total = jnp.sum(current, axis=0)
    local_peak = jnp.max(current, axis=0)
    summed = lax.psum(local_total, "pair")
    largest = lax.pmax(local_peak, "pair")
    return (voltage, summed, largest)


def solution(mesh):
    in_specs = (P("row", "col"), P("row", "col"), P("pair", None), P("pair", "row", "col"))
    out_specs = (P("pair", "row", "col"), P("row", "col"), P("row", "col"))
    return jax.shard_map(
        on_device, mesh=mesh, in_specs=in_specs, out_specs=out_specs, check_vma=False
    )
```

profile of v0, /device:TPU:1, one launch (start us, length us, event | category | flops | bytes accessed | tf_op | source)
XLA Modules:
  0.0 1850.5 jit_solution(10316426714045098077)
XLA Ops:
  8.1 4.0 collective-permute-start.4
  14.7 4.1 collective-permute-start
  23.3 5.7 collective-permute-start.2
  31.1 3.6 collective-permute-start.6
  39.1 3.4 collective-permute-done.7
  43.5 3.2 collective-permute-start.8
  48.1 4.3 collective-permute-done.9
  58.8 4.4 collective-permute-done.11
  65.2 133.5 %all-reduce = (f32[2]{0:T(128)S(1)}, f32[2]{0:T(128)S(1)}) all-reduce(f32[2]{0:T(128)S(1)} %get-tuple-element.6, f32[2]{0:T(128)S(1)} %get-tuple-element.5), channel_id=1, replica_groups=mesh['pair'=4,'row'=8,'col'=8] {'row','col'}, use_global_device_ids=true, to_apply=%region_1.0 | all-reduce | flops 4 | bytes 32 | tf_op jit(solution)/shard_map/psum | solution.py:70
  201.5 143.2 %psum.93 = f32[2]{0:T(128)S(1)} all-reduce(f32[2]{0:T(128)S(1)} %get-tuple-element.25), channel_id=1, replica_groups=mesh['pair'=4,'row'=8,'col'=8] {'row','col'}, use_global_device_ids=true, to_apply=%region_5.0 | all-reduce | flops 2 | bytes 16 | tf_op jit(solution)/shard_map/psum | solution.py:70
  354.3 3.1 collective-permute-start.15
  357.7 4.4 collective-permute-done.15
  364.0 134.6 %psum.94 = f32[2]{0:T(128)S(1)} all-reduce(f32[2]{0:T(128)S(1)} %get-tuple-element.23), channel_id=1, replica_groups=mesh['pair'=4,'row'=8,'col'=8] {'row','col'}, use_global_device_ids=true, to_apply=%region_7.0 | all-reduce | flops 2 | bytes 16 | tf_op jit(solution)/shard_map/psum | solution.py:98
  501.5 142.1 %psum.95 = f32[2]{0:T(128)S(1)} all-reduce(f32[2]{0:T(128)S(1)} %get-tuple-element.21), channel_id=1, replica_groups=mesh['pair'=4,'row'=8,'col'=8] {'row','col'}, use_global_device_ids=true, to_apply=%region_9.0 | all-reduce | flops 2 | bytes 16 | tf_op jit(solution)/shard_map/psum | solution.py:70
  656.6 4.4 collective-permute-done.19
  662.9 134.6 %psum.96 = f32[2]{0:T(128)S(1)} all-reduce(f32[2]{0:T(128)S(1)} %get-tuple-element.19), channel_id=1, replica_groups=mesh['pair'=4,'row'=8,'col'=8] {'row','col'}, use_global_device_ids=true, to_apply=%region_11.0 | all-reduce | flops 2 | bytes 16 | tf_op jit(solution)/shard_map/psum | solution.py:98
  800.3 142.1 %psum.97 = f32[2]{0:T(128)S(1)} all-reduce(f32[2]{0:T(128)S(1)} %get-tuple-element.17), channel_id=1, replica_groups=mesh['pair'=4,'row'=8,'col'=8] {'row','col'}, use_global_device_ids=true, to_apply=%region_13.0 | all-reduce | flops 2 | bytes 16 | tf_op jit(solution)/shard_map/psum | solution.py:70
  952.0 3.1 collective-permute-start.23
  955.4 4.4 collective-permute-done.23
  961.7 134.6 %psum.98 = f32[2]{0:T(128)S(1)} all-reduce(f32[2]{0:T(128)S(1)} %get-tuple-element.15), channel_id=1, replica_groups=mesh['pair'=4,'row'=8,'col'=8] {'row','col'}, use_global_device_ids=true, to_apply=%region_15.0 | all-reduce | flops 2 | bytes 16 | tf_op jit(solution)/shard_map/psum | solution.py:98
  1099.1 142.1 %psum.99 = f32[2]{0:T(128)S(1)} all-reduce(f32[2]{0:T(128)S(1)} %get-tuple-element.13), channel_id=1, replica_groups=mesh['pair'=4,'row'=8,'col'=8] {'row','col'}, use_global_device_ids=true, to_apply=%region_17.0 | all-reduce | flops 2 | bytes 16 | tf_op jit(solution)/shard_map/psum | solution.py:70
  1250.8 3.1 collective-permute-start.27
  1254.2 4.4 collective-permute-done.27
  1260.5 134.6 %psum.100 = f32[2]{0:T(128)S(1)} all-reduce(f32[2]{0:T(128)S(1)} %get-tuple-element.11), channel_id=1, replica_groups=mesh['pair'=4,'row'=8,'col'=8] {'row','col'}, use_global_device_ids=true, to_apply=%region_19.0 | all-reduce | flops 2 | bytes 16 | tf_op jit(solution)/shard_map/psum | solution.py:98
  1397.1 142.1 %psum.101 = f32[2]{0:T(128)S(1)} all-reduce(f32[2]{0:T(128)S(1)} %fusion.4), channel_id=1, replica_groups=mesh['pair'=4,'row'=8,'col'=8] {'row','col'}, use_global_device_ids=true, to_apply=%region_21.0 | all-reduce | flops 2 | bytes 16 | tf_op jit(solution)/shard_map/psum | solution.py:70
  1549.3 3.1 collective-permute-start.31
  1552.7 4.4 collective-permute-done.31
  1558.1 134.6 %psum.102 = f32[2]{0:T(128)S(1)} all-reduce(f32[2]{0:T(128)S(1)} %fusion.25), channel_id=1, replica_groups=mesh['pair'=4,'row'=8,'col'=8] {'row','col'}, use_global_device_ids=true, to_apply=%region_23.0 | all-reduce | flops 2 | bytes 16 | tf_op jit(solution)/shard_map/psum | solution.py:98
  1692.7 4.1 multiply_add_fusion.5
  1705.1 6.2 collective-permute-start.35
  1715.6 69.6 %all-reduce.6.cloned.1.call-done = f32[256,512]{1,0:T(8,128)} async-done(((f32[256,512]{1,0:T(8,128)}), f32[256,512]{1,0:T(8,128)}) %all-reduce.6.cloned.1.call-update) | async-done | bytes 524304 | tf_op jit(solution)/shard_map/pmax | solution.py:110
  1785.2 55.8 %all-reduce.4.cloned.1.call-done = f32[256,512]{1,0:T(8,128)} async-done(((f32[256,512]{1,0:T(8,128)}), f32[256,512]{1,0:T(8,128)}) %all-reduce.4.cloned.1.call-update) | async-done | bytes 524304 | tf_op jit(solution)/shard_map/psum | solution.py:109
  (145 shorter events, 114.9 us)
Async XLA Ops:
  7.2 1778.0 %all-reduce.6.cloned.1.call-start = ((), (), s32[]{:S(2)}) async-start(), calls=%async_computation.1 | async-start | bytes 1048576 | tf_op jit(solution)/shard_map/pmax | solution.py:110
  8.1 22.8 %collective-permute-start.4 = (f32[2,1,512]{2,1,0:T(1,128)S(1)}, f32[2,1,512]{2,1,0:T(1,128)S(1)}, u32[]{:S(2)}, u32[]{:S(2)}) collective-permute-start(f32[2,1,512]{2,1,0:T(1,128)S(1)} %get-tuple-element.69), channel_id=1, source_target_pairs={{0,8},{8,16},{16,24},{24,32},{32,40},{40,48},{48,56},{1,9},{9,17},... | collective-permute-start | bytes 12296 | tf_op jit(solution)/shard_map/ppermute | solution.py:17
  12.1 18.8 %collective-permute-start.5 = (f32[2,1,512]{2,1,0:T(1,128)S(1)}, f32[2,1,512]{2,1,0:T(1,128)S(1)}, u32[]{:S(2)}, u32[]{:S(2)}) collective-permute-start(f32[2,1,512]{2,1,0:T(1,128)S(1)} %get-tuple-element.70), channel_id=1, source_target_pairs={{8,0},{16,8},{24,16},{32,24},{40,32},{48,40},{56,48},{9,1},{17,9},... | collective-permute-start | bytes 12296 | tf_op jit(solution)/shard_map/ppermute | solution.py:20
  14.7 5.8 collective-permute-start
  18.8 4.4 collective-permute-start.1
  23.3 13.4 collective-permute-start.2
  29.0 7.8 collective-permute-start.3
  31.1 8.0 collective-permute-start.6
  34.7 7.8 collective-permute-start.7
  43.5 4.5 collective-permute-start.8
  46.8 5.6 collective-permute-start.9
  52.5 6.3 collective-permute-start.10
  55.4 7.8 collective-permute-start.11
  347.9 4.4 collective-permute-start.13
  352.4 5.3 collective-permute-start.14
  354.3 7.8 collective-permute-start.15
  646.7 4.4 collective-permute-start.17
  651.3 5.3 collective-permute-start.18
  653.2 7.8 collective-permute-start.19
  945.6 4.4 collective-permute-start.21
  950.1 5.3 collective-permute-start.22
  952.0 7.8 collective-permute-start.23
  1244.4 4.4 collective-permute-start.25
  1248.9 5.3 collective-permute-start.26
  1250.8 7.8 collective-permute-start.27
  1542.8 4.4 collective-permute-start.29
  1547.4 5.3 collective-permute-start.30
  1549.3 7.8 collective-permute-start.31
  1698.1 4.4 collective-permute-start.33
  1702.6 8.7 collective-permute-start.34
  1705.1 7.8 collective-permute-start.35
  1714.8 126.1 %all-reduce.4.cloned.1.call-start = ((), (), s32[]{:S(2)}) async-start(), calls=%async_computation | async-start | bytes 1048576 | tf_op jit(solution)/shard_map/psum | solution.py:109
  (20 other events, 260.8 us)
Sparse Core Ops, SparseCore 0:
  1715.0 70.1 all-reduce.5
  1788.4 52.5 all-reduce.3
where the time goes:
time: 1850 us
  blocking collectives  1520 us (82%)
  waiting for transfers between devices  185 us (10%)
  starting transfers between devices  82.7 us (4%)
  other arithmetic  45.5 us (2%)
    psum x6, blocking collectives, squared_progress(): return lax.psum(jnp.sum(residual * scaled, axis=(1, 2)), ('row', 'col'))  845 us
    psum x5, blocking collectives, on_device(): curve = lax.psum(jnp.sum(search * image, axis=(1, 2)), ('row', 'col'))  673 us
    pmax x1, waiting for transfers between devices, on_device(): largest = lax.pmax(local_peak, 'pair')  69.6 us
    ppermute x18, waiting for transfers between devices, padded_2(): lax.ppermute(lax.slice_in_dim(block, 0, width, axis=dim), axis, backward)  56.5 us
    psum x1, waiting for transfers between devices, on_device(): summed = lax.psum(local_total, 'pair')  55.8 us
    ppermute x18, starting transfers between devices, padded_2(): lax.ppermute(lax.slice_in_dim(block, block.shape[dim] - width, None, axis...  43.4 us
    ppermute x18, starting transfers between devices, padded_2(): lax.ppermute(lax.slice_in_dim(block, 0, width, axis=dim), axis, backward)  39.2 us
  transfers between devices with their start and end apart: 38, of which 25 were waited for; matrix products, arithmetic and copies ran while one was open for 0% of the time, Pallas kernels for 0%

commit v1 on v0

v1 whole, which is shorter than its diff:
```python
import functools

import jax
import jax.numpy as jnp
from jax import lax
from jax.experimental import pallas as pl
from jax.experimental.pallas import tpu as pltpu
from jax.sharding import PartitionSpec as P

MESH = pl.DeviceIdType.MESH
LEAKAGE = 0.01
STEPS = 6
LANES = 128
EDGE = 8
OWN = 16
HIGH = jax.lax.Precision.HIGHEST


def lane_ids():
    return lax.broadcasted_iota(jnp.int32, (8, LANES), 1)


def east(tiles):
    last = lane_ids() == LANES - 1
    rolled = [pltpu.roll(tile, LANES - 1, 1) for tile in tiles]
    return [jnp.where(last, rolled[(t + 1) % len(tiles)], rolled[t]) for t in range(len(tiles))]


def west(tiles):
    first = lane_ids() == 0
    rolled = [pltpu.roll(tile, 1, 1) for tile in tiles]
    return [jnp.where(first, rolled[t - 1], rolled[t]) for t in range(len(tiles))]


def link(a, b):
    return jnp.where(jnp.minimum(a, b) > 0.0, 0.5 * (a + b), 0.0)


def solve_coefficients(totals):
    same = [totals[2 * k] for k in range(STEPS)]
    after = [totals[2 * k + 1] for k in range(STEPS)]
    nu = [same[1], after[1]]
    for k in range(1, STEPS - 1):
        nu.append(2.0 * same[k + 1] - nu[0])
        nu.append(2.0 * after[k + 1] - nu[1])
    rho = [same[0], after[0], nu[0]]
    for k in range(1, STEPS - 2):
        rho.append(2.0 * nu[k] - rho[k])
    gram = [[None] * STEPS for _ in range(STEPS)]
    gram[0][0] = rho[0] - rho[1]
    for j in range(1, STEPS):
        gram[0][j] = rho[j] - nu[j - 1]
    for i in range(STEPS - 1):
        for j in range(i, STEPS - 1):
            before = abs(j - 1)
            gram[i + 1][j + 1] = 0.5 * (nu[i + j] + nu[abs(i - j)]) - 0.25 * (
                nu[i + j + 1] + nu[abs(i - j - 1)] + nu[i + before] + nu[abs(i - before)]
            )
    right = list(rho)
    least = [3e-7 * gram[j][j] for j in range(STEPS)]
    inverse, factors = [], {}
    for j in range(STEPS):
        pivot = gram[j][j]
        usable = pivot > least[j]
        inverse.append(jnp.where(usable, 1.0 / jnp.where(usable, pivot, 1.0), 0.0))
        for i in range(j + 1, STEPS):
            factors[i, j] = gram[j][i] * inverse[j]
        for i in range(j + 1, STEPS):
            for m in range(i, STEPS):
                gram[i][m] = gram[i][m] - factors[i, j] * gram[j][m]
            right[i] = right[i] - factors[i, j] * right[j]
    out = [right[j] * inverse[j] for j in range(STEPS)]
    for i in reversed(range(STEPS)):
        for j in range(i + 1, STEPS):
            out[i] = out[i] - factors[j, i] * out[j]
    return out


def kernel(
    sizes,
    cond_in,
    mask_in,
    focal,
    volts_in,
    volts_out,
    sum_out,
    max_out,
    stage_cond,
    stage_mask,
    volts,
    cond,
    link_e,
    link_n,
    scale,
    coef_c,
    coef_e,
    coef_n,
    basis,
    pack_e,
    pack_w,
    land_w,
    land_e,
    dots,
    message,
    gather_col,
    gather_row,
    local,
    far,
    from_prev,
    from_next,
    result,
    load_sem,
    store_sem,
    halo_send,
    halo_recv,
    red_send,
    red_recv,
    ring_send,
    ring_recv,
):
    pairs, rows, tiles, n_pair, n_row, n_col = sizes
    wide = tiles + 1
    chunks = rows // 8
    fold = rows // 4
    fold_chunks = fold // 8
    quarter = rows // 4
    unit = quarter // 4
    my_pair, my_row, my_col = lax.axis_index("pair"), lax.axis_index("row"), lax.axis_index("col")

    def around(index, step, count):
        return lax.rem(index + (step + count), count)

    loads = []
    for t in range(tiles):
        lanes = pl.ds(t * LANES, LANES)
        loads.append(pltpu.make_async_copy(cond_in.at[:, lanes], stage_cond.at[t], load_sem.at[len(loads)]))
        loads.append(pltpu.make_async_copy(mask_in.at[:, lanes], stage_mask.at[t], load_sem.at[len(loads)]))
        for p in range(pairs):
            loads.append(
                pltpu.make_async_copy(
                    volts_in.at[p, :, lanes], volts.at[p, t, pl.ds(OWN, rows)], load_sem.at[len(loads)]
                )
            )
    for load in loads:
        load.start()

    north, south = around(my_row, -1, n_row), around(my_row, 1, n_row)
    westward, eastward = around(my_col, -1, n_col), around(my_col, 1, n_col)
    before, after = around(my_pair, -1, n_pair), around(my_pair, 1, n_pair)
    partners = [{"col": around(my_col, step, n_col)} for step in range(1, n_col)]
    partners += [{"row": around(my_row, step, n_row)} for step in range(1, n_row)]
    partners += [{"row": r, "col": c} for r in (north, south) for c in (westward, eastward)]
    partners += [{"pair": before}, {"pair": after}]
    barrier = pltpu.get_barrier_semaphore()
    for partner in partners:
        pl.semaphore_signal(barrier, inc=1, device_id=partner, device_id_type=MESH)

    zero = jnp.zeros((8, LANES), jnp.float32)
    for start in (0, rows + 3 * 8):
        at = pl.ds(start, 8)
        for t in range(wide):
            for ref in (cond, scale, link_n, coef_n):
                ref[t, at, :] = zero
            for p in range(pairs):
                volts[p, t, at, :] = zero
                for k in range(STEPS):
                    basis[k, p, t, at, :] = zero

    for load in loads:
        load.wait()

    def own_cond(c, carry):
        at = pl.ds(pl.multiple_of(8 * c, 8), 8)
        to = pl.ds(pl.multiple_of(OWN + 8 * c, 8), 8)
        for t in range(tiles):
            cond[t, to, :] = stage_cond[t, at, :] * stage_mask[t, at, :].astype(jnp.float32)
        return carry

    lax.fori_loop(0, chunks, own_cond, 0)

    lane = lane_ids()

    def pack(c, carry):
        for side, tile, ref in ((0, 0, pack_w), (1, tiles - 1, pack_e)):
            packed = jnp.zeros((8, LANES), jnp.float32)
            for g in range(4):
                at = pl.ds(pl.multiple_of(OWN + g * fold + 8 * c, 8), 8)
                fields = [volts[p, tile, at, :] for p in range(pairs)] + [cond[tile, at, :]]
                for f, value in enumerate(fields):
                    low = 32 * g + 8 * f
                    first = 0 if side == 0 else LANES - 8
                    shift = (low - first) % LANES
                    moved = pltpu.roll(value, shift, 1) if shift else value
                    packed = jnp.where((lane >= low) & (lane < low + 8), moved, packed)
            ref[pl.ds(pl.multiple_of(8 * c, 8), 8), :] = packed
        return carry

    lax.fori_loop(0, fold_chunks, pack, 0)
    pl.semaphore_wait(barrier, len(partners))

    top, bottom = pl.ds(OWN, 8), pl.ds(OWN + rows - 8, 8)
    over, under = pl.ds(OWN - 8, 8), pl.ds(OWN + rows, 8)
    mid = pl.ds(8, fold)
    halo = [
        (volts.at[:, pl.ds(0, tiles), top], volts.at[:, pl.ds(0, tiles), under], {"row": north}),
        (cond.at[pl.ds(0, tiles), top], cond.at[pl.ds(0, tiles), under], {"row": north}),
        (volts.at[:, pl.ds(0, tiles), bottom], volts.at[:, pl.ds(0, tiles), over], {"row": south}),
        (cond.at[pl.ds(0, tiles), bottom], cond.at[pl.ds(0, tiles), over], {"row": south}),
        (pack_w, land_e.at[mid], {"col": westward}),
        (pack_e, land_w.at[mid], {"col": eastward}),
        (pack_w.at[pl.ds(0, 8)], land_e.at[pl.ds(fold + 8, 8)], {"row": north, "col": westward}),
        (pack_w.at[pl.ds(fold - 8, 8)], land_e.at[pl.ds(0, 8)], {"row": south, "col": westward}),
        (pack_e.at[pl.ds(0, 8)], land_w.at[pl.ds(fold + 8, 8)], {"row": north, "col": eastward}),
        (pack_e.at[pl.ds(fold - 8, 8)], land_w.at[pl.ds(0, 8)], {"row": south, "col": eastward}),
    ]
    halo = [
        pltpu.make_async_remote_copy(
            src_ref=src,
            dst_ref=dst,
            send_sem=halo_send.at[i],
            recv_sem=halo_recv.at[i],
            device_id=who,
            device_id_type=MESH,
        )
        for i, (src, dst, who) in enumerate(halo)
    ]
    for copy in halo:
        copy.start()
    for copy in halo:
        copy.wait()

    has_n = (my_row > 0).astype(jnp.float32)
    has_s = (my_row < n_row - 1).astype(jnp.float32)
    has_w = (my_col > 0).astype(jnp.float32)
    has_e = (my_col < n_col - 1).astype(jnp.float32)
    for t in range(tiles):
        cond[t, over, :] = cond[t, over, :] * has_n
        cond[t, under, :] = cond[t, under, :] * has_s

    def unpack(source, g, to, keep):
        left = land_w[source, :]
        right = land_e[source, :]
        for f in range(pairs + 1):
            low = 32 * g + 8 * f
            a = pltpu.roll(left, (LANES - 8 - low) % LANES, 1)
            b = pltpu.roll(right, (LANES - low) % LANES, 1) if low else right
            if f == pairs:
                a, b = a * (has_w * keep), b * (has_e * keep)
            value = jnp.where(lane < 8, b, jnp.where(lane >= LANES - 8, a, 0.0))
            if f == pairs:
                cond[tiles, to, :] = value
            else:
                volts[f, tiles, to, :] = value

    def unpack_chunk(c, carry):
        for g in range(4):
            unpack(
                pl.ds(pl.multiple_of(8 + 8 * c, 8), 8),
                g,
                pl.ds(pl.multiple_of(OWN + g * fold + 8 * c, 8), 8),
                1.0,
            )
        return carry

    lax.fori_loop(0, fold_chunks, unpack_chunk, 0)
    unpack(pl.ds(0, 8), 3, over, has_n)
    unpack(pl.ds(fold + 8, 8), 0, under, has_s)

    def links_chunk(c, carry):
        start = pl.multiple_of(8 + 8 * c, 8)
        at = pl.ds(start, 8)
        here = [cond[t, at, :] for t in range(wide)]
        right = [link(a, b) for a, b in zip(here, east(here))]
        left = west(right)
        for t in range(wide):
            up = link(here[t], cond[t, pl.ds(start - 1, 8), :])
            down = link(here[t], cond[t, pl.ds(start + 1, 8), :])
            diagonal = up + down + left[t] + right[t] + LEAKAGE * here[t] + jnp.where(here[t] > 0.0, 0.0, 1.0)
            most = jnp.maximum(diagonal, 1.0)
            root = lax.rsqrt(most)
            root = root * (1.5 - 0.5 * most * root * root)
            link_e[t, at, :] = right[t]
            link_n[t, at, :] = up
            scale[t, at, :] = root
            coef_c[t, at, :] = 2.0 * jnp.maximum(1.0 - diagonal, 0.0)
        return carry

    lax.fori_loop(0, chunks + 2, links_chunk, 0)

    width_all = tiles * LANES * n_col
    sub = lax.broadcasted_iota(jnp.int32, (8, LANES), 0)
    columns = [my_col * (tiles * LANES) + t * LANES + lane for t in range(tiles)]
    columns.append(my_col * (tiles * LANES) + jnp.where(lane < 64, tiles * LANES, -LANES) + lane)

    def start_chunk(c, carry):
        start = pl.multiple_of(8 + 8 * c, 8)
        at, up_at, down_at = pl.ds(start, 8), pl.ds(start - 1, 8), pl.ds(start + 1, 8)
        root = [scale[t, at, :] for t in range(wide)]
        right = [link_e[t, at, :] for t in range(wide)]
        up = [link_n[t, at, :] for t in range(wide)]
        root_e = east(root)
        flat = (my_row * rows + 8 * c - 8 + sub) * width_all
        own = []
        for t in range(wide):
            coef_e[t, at, :] = 2.0 * right[t] * root[t] * root_e[t]
            coef_n[t, at, :] = 2.0 * up[t] * root[t] * scale[t, up_at, :]
            value = cond[t, at, :]
            own.append(LEAKAGE * value + jnp.where(value > 0.0, 0.0, 1.0))
        for p in range(pairs):
            here = [volts[p, t, at, :] for t in range(wide)]
            there = east(here)
            flow = [right[t] * (here[t] - there[t]) for t in range(wide)]
            flow_w = west(flow)
            for t in range(wide):
                total = flow[t] - flow_w[t] + own[t] * here[t]
                total = total + up[t] * (here[t] - volts[p, t, up_at, :])
                total = total + link_n[t, down_at, :] * (here[t] - volts[p, t, down_at, :])
                cell = flat + columns[t]
                inject = jnp.where(cell == focal[p, 0], 1.0, 0.0) - jnp.where(cell == focal[p, 1], 1.0, 0.0)
                basis[0, p, t, at, :] = root[t] * (inject - total)
        return carry

    lax.fori_loop(0, chunks + 2, start_chunk, 0)

    def advance(k, c, sums):
        start = pl.multiple_of(8 + 8 * c, 8)
        at, up_at, down_at = pl.ds(start, 8), pl.ds(start - 1, 8), pl.ds(start + 1, 8)
        final = k == STEPS - 1
        count = tiles if final else wide
        right = [coef_e[t, at, :] for t in range(wide)]
        out = []
        for p in range(pairs):
            here = [basis[k, p, t, at, :] for t in range(wide)]
            there = east(here)
            back = west([right[t] * here[t] for t in range(wide)])
            same = jnp.zeros((8, LANES), jnp.float32)
            step = jnp.zeros((8, LANES), jnp.float32)
            for t in range(count):
                value = coef_c[t, at, :] * here[t] + right[t] * there[t] + back[t]
                value = value + coef_n[t, at, :] * basis[k, p, t, up_at, :]
                value = value + coef_n[t, down_at, :] * basis[k, p, t, down_at, :]
                value = 0.5 * value if k < 2 else value - basis[k - 1, p, t, at, :]
                if not final:
                    basis[k + 1, p, t, at, :] = value
                if sums is not None and t < tiles:
                    same = same + here[t] * here[t]
                    step = step + here[t] * value
            if sums is not None:
                out += [sums[2 * p] + same, sums[2 * p + 1] + step]
        return tuple(out)

    for k in range(STEPS):
        if k < STEPS - 1:

            def border(i, carry, k=k):
                advance(k, i * (chunks + 1), None)
                return carry

            lax.fori_loop(0, 2, border, 0)
        sums = lax.fori_loop(1, chunks + 1, functools.partial(advance, k), (zero,) * (2 * pairs))
        for p in range(pairs):
            dots[(2 * k) * pairs + p] = sums[2 * p]
            dots[(2 * k + 1) * pairs + p] = sums[2 * p + 1]

    n_dots = 2 * STEPS * pairs
    part = jnp.sum(dots[...], axis=1)
    message[...] = jnp.broadcast_to(jnp.sum(part, axis=1, keepdims=True), (n_dots, LANES))

    def reduce_over(axis, me, count, source, gather, phase):
        copies = []
        for step in range(1, count):
            copies.append(
                pltpu.make_async_remote_copy(
                    src_ref=source,
                    dst_ref=gather.at[me],
                    send_sem=red_send.at[phase, step - 1],
                    recv_sem=red_recv.at[phase, step - 1],
                    device_id={axis: around(me, step, count)},
                    device_id_type=MESH,
                )
            )
        for copy in copies:
            copy.start()
        gather[me] = source[...]
        for copy in copies:
            copy.wait()
        total = gather[0]
        for i in range(1, count):
            total = total + gather[i]
        return total

    message[...] = reduce_over("col", my_col, n_col, message, gather_col, 0)
    totals = reduce_over("row", my_row, n_row, message, gather_row, 1)
    parts = solve_coefficients([totals[j * pairs : (j + 1) * pairs] for j in range(2 * STEPS)])
    weights = [[jnp.broadcast_to(part[p : p + 1], (8, LANES)) for part in parts] for p in range(pairs)]

    def volts_chunk(c, carry):
        at = pl.ds(pl.multiple_of(8 + 8 * c, 8), 8)
        for t in range(wide):
            root = scale[t, at, :]
            for p in range(pairs):
                change = weights[p][0] * basis[0, p, t, at, :]
                for k in range(1, STEPS):
                    change = change + weights[p][k] * basis[k, p, t, at, :]
                volts[p, t, at, :] = volts[p, t, at, :] + root * change
        return carry

    lax.fori_loop(0, chunks + 2, volts_chunk, 0)
    stores = []
    for t in range(tiles):
        for p in range(pairs):
            stores.append(
                pltpu.make_async_copy(
                    volts.at[p, t, pl.ds(OWN, rows)],
                    volts_out.at[p, :, pl.ds(t * LANES, LANES)],
                    store_sem.at[len(stores)],
                )
            )
    for store in stores:
        store.start()

    def currents(index):
        def body(i, carry):
            row = index * quarter + 8 * i
            start = pl.multiple_of(OWN + row, 8)
            at, up_at, down_at = pl.ds(start, 8), pl.ds(start - 1, 8), pl.ds(start + 1, 8)
            right = [link_e[t, at, :] for t in range(wide)]
            total, peak = [None] * tiles, [None] * tiles
            for p in range(pairs):
                here = [volts[p, t, at, :] for t in range(wide)]
                there = east(here)
                flow = [jnp.abs(right[t] * (here[t] - there[t])) for t in range(wide)]
                flow_w = west(flow)
                for t in range(tiles):
                    value = flow[t] + flow_w[t]
                    value = value + jnp.abs(link_n[t, at, :] * (here[t] - volts[p, t, up_at, :]))
                    value = value + jnp.abs(link_n[t, down_at, :] * (here[t] - volts[p, t, down_at, :]))
                    value = 0.5 * value
                    total[t] = value if p == 0 else total[t] + value
                    peak[t] = value if p == 0 else jnp.maximum(peak[t], value)
            to = pl.ds(pl.multiple_of(row, 8), 8)
            for t in range(tiles):
                local[0, to, pl.ds(t * LANES, LANES)] = total[t]
                local[1, to, pl.ds(t * LANES, LANES)] = peak[t]
            return carry

        lax.fori_loop(0, quarter // 8, body, 0)

    q_next, q_prev = around(my_pair, 1, n_pair), around(my_pair, -1, n_pair)
    q_far = around(my_pair, 2, n_pair)

    def span(index, u):
        return pl.ds(pl.multiple_of(index * quarter + u * unit, unit), unit)

    def ring(slot, src, dst, who):
        copy = pltpu.make_async_remote_copy(
            src_ref=src,
            dst_ref=dst,
            send_sem=ring_send.at[slot],
            recv_sem=ring_recv.at[slot],
            device_id={"pair": who},
            device_id_type=MESH,
        )
        copy.start()
        return copy

    in_unit = [pl.ds(u * unit, unit) for u in range(4)]
    sent = {}
    currents(q_far)
    for i in range(2):
        sent["far", i] = ring(i, local.at[:, span(q_far, i)], far.at[:, in_unit[i]], q_next)
        sent["far", 2 + i] = ring(2 + i, local.at[:, span(q_far, 2 + i)], far.at[:, in_unit[2 + i]], q_prev)
    currents(q_next)
    for u in (2, 3):
        sent["prev", u] = ring(4 + u, local.at[:, span(q_next, u)], from_prev.at[:, in_unit[u]], q_next)
    currents(q_prev)
    for u in (0, 1):
        sent["next", u] = ring(8 + u, local.at[:, span(q_prev, u)], from_next.at[:, in_unit[u]], q_prev)
    currents(my_pair)
    for i in range(2):
        for u, owner, name, base, target in (
            (i, q_next, "prev", 4, from_prev),
            (2 + i, q_prev, "next", 8, from_next),
        ):
            sent["far", u].wait_recv()
            at = span(owner, u)
            local[0, at, :] = local[0, at, :] + far[0, in_unit[u], :]
            local[1, at, :] = jnp.maximum(local[1, at, :], far[1, in_unit[u], :])
            sent[name, u] = ring(base + u, local.at[:, at], target.at[:, in_unit[u]], owner)
    for u in (0, 2, 1, 3):
        sent["prev", u].wait_recv()
        sent["next", u].wait_recv()
        at = span(my_pair, u)
        result[0, at, :] = local[0, at, :] + from_prev[0, in_unit[u], :] + from_next[0, in_unit[u], :]
        result[1, at, :] = jnp.maximum(
            local[1, at, :], jnp.maximum(from_prev[1, in_unit[u], :], from_next[1, in_unit[u], :])
        )
        sent["up", u] = ring(12 + u, result.at[:, at], result.at[:, at], q_next)
        sent["down", u] = ring(16 + u, result.at[:, at], result.at[:, at], q_prev)
    for i in range(2):
        sent["up", i].wait_recv()
        at = span(q_prev, i)
        sent["over", i] = ring(20 + i, result.at[:, at], result.at[:, at], q_next)
        sent["down", 2 + i].wait_recv()
        at = span(q_next, 2 + i)
        sent["over", 2 + i] = ring(22 + i, result.at[:, at], result.at[:, at], q_prev)
    for i in range(2):
        sent["up", 2 + i].wait_recv()
        sent["down", i].wait_recv()

    def keep(index, number):
        at = pl.ds(pl.multiple_of(index * quarter, quarter), quarter)
        base = pairs * tiles + 2 * number
        for i, ref in enumerate((sum_out, max_out)):
            stores.append(pltpu.make_async_copy(result.at[i, at], ref.at[at], store_sem.at[base + i]))
            stores[-1].start()

    keep(my_pair, 0)
    keep(q_prev, 1)
    keep(q_next, 2)
    for u in range(4):
        sent["over", u].wait_recv()
    keep(q_far, 3)
    for copy in sent.values():
        copy.wait_send()
    for store in stores:
        store.wait()


def on_device(mesh_sizes, conductance, valid_mask, focal_cells, initial_volts):
    rows, columns = conductance.shape
    pairs = initial_volts.shape[0]
    tiles = columns // LANES
    n_pair, n_row, n_col = mesh_sizes
    sizes = (pairs, rows, tiles, n_pair, n_row, n_col)
    wide, tall, fold, quarter = tiles + 1, rows + 32, rows // 4, rows // 4
    n_dots = 2 * STEPS * pairs
    f32 = jnp.float32
    anywhere = pl.BlockSpec(memory_space=pl.ANY)
    field = pltpu.VMEM((wide, tall, LANES), f32)
    return pl.pallas_call(
        functools.partial(kernel, sizes),
        out_shape=(
            jax.ShapeDtypeStruct((pairs, rows, columns), f32),
            jax.ShapeDtypeStruct((rows, columns), f32),
            jax.ShapeDtypeStruct((rows, columns), f32),
        ),
        in_specs=[anywhere, anywhere, pl.BlockSpec(memory_space=pltpu.SMEM), anywhere],
        out_specs=(anywhere, anywhere, anywhere),
        scratch_shapes=[
            pltpu.VMEM((tiles, rows, LANES), f32),
            pltpu.VMEM((tiles, rows, LANES), jnp.int32),
            pltpu.VMEM((pairs, wide, tall, LANES), f32),
            field,
            field,
            field,
            field,
            field,
            field,
            field,
            pltpu.VMEM((STEPS, pairs, wide, tall, LANES), f32),
            pltpu.VMEM((fold, LANES), f32),
            pltpu.VMEM((fold, LANES), f32),
            pltpu.VMEM((fold + 16, LANES), f32),
            pltpu.VMEM((fold + 16, LANES), f32),
            pltpu.VMEM((n_dots, 8, LANES), f32),
            pltpu.VMEM((n_dots, LANES), f32),
            pltpu.VMEM((n_col, n_dots, LANES), f32),
            pltpu.VMEM((n_row, n_dots, LANES), f32),
            pltpu.VMEM((2, rows, columns), f32),
            pltpu.VMEM((2, quarter, columns), f32),
            pltpu.VMEM((2, quarter, columns), f32),
            pltpu.VMEM((2, quarter, columns), f32),
            pltpu.VMEM((2, rows, columns), f32),
            pltpu.SemaphoreType.DMA(((2 + pairs) * tiles,)),
            pltpu.SemaphoreType.DMA((pairs * tiles + 8,)),
            pltpu.SemaphoreType.DMA((10,)),
            pltpu.SemaphoreType.DMA((10,)),
            pltpu.SemaphoreType.DMA((2, max(n_col, n_row) - 1)),
            pltpu.SemaphoreType.DMA((2, max(n_col, n_row) - 1)),
            pltpu.SemaphoreType.DMA((24,)),
            pltpu.SemaphoreType.DMA((24,)),
        ],
        compiler_params=pltpu.CompilerParams(
            collective_id=0, has_side_effects=True, vmem_limit_bytes=48 * 1024 * 1024
        ),
    )(conductance, valid_mask, focal_cells, initial_volts)


def solution(mesh):
    in_specs = (P("row", "col"), P("row", "col"), P("pair", None), P("pair", "row", "col"))
    out_specs = (P("pair", "row", "col"), P("row", "col"), P("row", "col"))
    sizes = (mesh.shape["pair"], mesh.shape["row"], mesh.shape["col"])
    return jax.shard_map(
        functools.partial(on_device, sizes), mesh=mesh, in_specs=in_specs, out_specs=out_specs, check_vma=False
    )
```

time: 1850 us -> 102 us (0.06)
  blocking collectives: 1520 us -> 0 us
  waiting for transfers between devices: 185 us -> 0 us
  Pallas kernels: 0 us -> 94.9 us
  starting transfers between devices: 82.7 us -> 0 us
  other arithmetic: 45.5 us -> 0 us
    psum x11 -> x0, blocking collectives: 1520 us -> none  [the longest x6 845 us: squared_progress(): return lax.psum(jnp.sum(residual * scaled, axis=(1, 2)), ('row', 'col'))]
    pallas_call x0 -> x1, Pallas kernels: none -> 94.9 us  [on_device(): pl.pallas_call(functools.partial(kernel, sizes), out_shape=(jax.ShapeDtyp...]
    ppermute x36 -> x0, starting transfers between devices: 82.6 us -> none  [the longest x18 43.4 us: padded_2(): lax.ppermute(lax.slice_in_dim(block, block.shape[dim] - width, None, axis...]
    pmax x1 -> x0, waiting for transfers between devices: 69.6 us -> none  [on_device(): largest = lax.pmax(local_peak, 'pair')]
    ppermute x36 -> x0, waiting for transfers between devices: 59.4 us -> none  [the longest x18 56.5 us: padded_2(): lax.ppermute(lax.slice_in_dim(block, 0, width, axis=dim), axis, backward)]
    psum x1 -> x0, waiting for transfers between devices: 55.8 us -> none  [on_device(): summed = lax.psum(local_total, 'pair')]
    reduce_sum x11 -> x0, other arithmetic: 23.9 us -> none  [the longest x5 13.2 us: squared_progress(): return lax.psum(jnp.sum(residual * scaled, axis=(1, 2)), ('row', 'col'))]
  transfers between devices with their start and end apart: 38 -> 0, of which waited for: 25 -> 0; matrix products, arithmetic and copies ran while one was open for 0% -> 0% of each run, Pallas kernels for 0% -> 0%
where the time goes in v1:
time: 102 us
  Pallas kernels  94.9 us (93%)
  local copies, waits for them, and re-layouts  6.54 us (6%)
    pallas_call x1, Pallas kernels, on_device(): pl.pallas_call(functools.partial(kernel, sizes), out_shape=(jax.ShapeDtyp...  94.9 us
    unnamed x11, local copies, waits for them, and re-layouts  6.54 us

profile of v1, /device:TPU:1, one launch (start us, length us, event | category | flops | bytes accessed | tf_op | source)
XLA Modules:
  0.0 102.1 jit_solution(6923070075756687573)
XLA Ops:
  0.6 0.0 copy-start
  0.6 1.2 %copy-done = f32[2,256,512]{2,1,0:T(8,128)S(1)} copy-done((f32[2,256,512]{2,1,0:T(8,128)S(1)}, f32[2,256,512]{2,1,0:T(8,128)}, u32[]{:S(2)}) %copy-start) | copy-done | bytes 1048600
  1.9 0.0 copy-start.1
  1.9 1.0 %copy-done.1 = f32[256,512]{1,0:T(8,128)S(1)} copy-done((f32[256,512]{1,0:T(8,128)S(1)}, f32[256,512]{1,0:T(8,128)}, u32[]{:S(2)}) %copy-start.1) | copy-done | bytes 524312
  2.9 0.0 copy-start.2
  2.9 1.0 %copy-done.2 = s32[256,512]{1,0:T(8,128)S(1)} copy-done((s32[256,512]{1,0:T(8,128)S(1)}, s32[256,512]{1,0:T(8,128)}, u32[]{:S(2)}) %copy-start.2) | copy-done | bytes 524312
  3.9 0.0 copy-start.3
  3.9 0.7 copy-done.3
  4.6 94.9 %shard_map.67 = (f32[2,256,512]{2,1,0:T(8,128)S(1)}, f32[256,512]{1,0:T(8,128)S(1)}, f32[256,512]{1,0:T(8,128)S(1)}) custom-call(f32[256,512]{1,0:T(8,128)S(1)} %copy-done.1, s32[256,512]{1,0:T(8,128)S(1)} %copy-done.2, s32[2,2]{1,0:T(2,128)S(1)} %copy-done.3, f32[2,256,512]{2,1,0:T(8,128)S(1)} %copy-done), custom_call_target="tpu_custom_call" | custom-call | tf_op jit(solution)/shard_map/pallas_call | solution.py:541
  99.5 1.0 copy.10
  100.5 0.8 copy.11
  101.3 0.8 copy.12
Async XLA Ops:
  0.6 1.2 %copy-start = (f32[2,256,512]{2,1,0:T(8,128)S(1)}, f32[2,256,512]{2,1,0:T(8,128)}, u32[]{:S(2)}) copy-start(f32[2,256,512]{2,1,0:T(8,128)} %volts_in.1) | copy-start | bytes 3145732
  1.9 1.0 %copy-start.1 = (f32[256,512]{1,0:T(8,128)S(1)}, f32[256,512]{1,0:T(8,128)}, u32[]{:S(2)}) copy-start(f32[256,512]{1,0:T(8,128)} %cond_in.1) | copy-start | bytes 1572868
  2.9 1.0 %copy-start.2 = (s32[256,512]{1,0:T(8,128)S(1)}, s32[256,512]{1,0:T(8,128)}, u32[]{:S(2)}) copy-start(s32[256,512]{1,0:T(8,128)} %mask_in.1) | copy-start | bytes 1572868
  3.9 0.7 copy-start.3

commit v2 on v1

--- a/solution.py
+++ b/solution.py
@@ -13,21 +13,21 @@
 LANES = 128
 EDGE = 8
 OWN = 16
-HIGH = jax.lax.Precision.HIGHEST
-
-
-def lane_ids():
-    return lax.broadcasted_iota(jnp.int32, (8, LANES), 1)
+BLOCK = 32
+
+
+def lane_ids(height):
+    return lax.broadcasted_iota(jnp.int32, (height, LANES), 1)
 
 
 def east(tiles):
-    last = lane_ids() == LANES - 1
+    last = lane_ids(tiles[0].shape[0]) == LANES - 1
     rolled = [pltpu.roll(tile, LANES - 1, 1) for tile in tiles]
     return [jnp.where(last, rolled[(t + 1) % len(tiles)], rolled[t]) for t in range(len(tiles))]
 
 
 def west(tiles):
-    first = lane_ids() == 0
+    first = lane_ids(tiles[0].shape[0]) == 0
     rolled = [pltpu.roll(tile, 1, 1) for tile in tiles]
     return [jnp.where(first, rolled[t - 1], rolled[t]) for t in range(len(tiles))]
 
@@ -178,7 +178,7 @@
 
     lax.fori_loop(0, chunks, own_cond, 0)
 
-    lane = lane_ids()
+    lane = lane_ids(8)
 
     def pack(c, carry):
         for side, tile, ref in ((0, 0, pack_w), (1, tiles - 1, pack_e)):
@@ -266,15 +266,26 @@
     unpack(pl.ds(0, 8), 3, over, has_n)
     unpack(pl.ds(fold + 8, 8), 0, under, has_s)
 
-    def links_chunk(c, carry):
-        start = pl.multiple_of(8 + 8 * c, 8)
-        at = pl.ds(start, 8)
+    def sweep_own(body, carry=()):
+        def step(c, carry):
+            return body(pl.multiple_of(OWN + BLOCK * c, 8), BLOCK, carry)
+
+        return lax.fori_loop(0, rows // BLOCK, step, carry)
+
+    def sweep_border(body):
+        def step(i, carry):
+            return body(pl.multiple_of(OWN - 8 + i * (rows + 8), 8), 8, carry)
+
+        lax.fori_loop(0, 2, step, ())
+
+    def links_rows(start, height, carry):
+        at = pl.ds(start, height)
         here = [cond[t, at, :] for t in range(wide)]
         right = [link(a, b) for a, b in zip(here, east(here))]
         left = west(right)
         for t in range(wide):
-            up = link(here[t], cond[t, pl.ds(start - 1, 8), :])
-            down = link(here[t], cond[t, pl.ds(start + 1, 8), :])
+            up = link(here[t], cond[t, pl.ds(start - 1, height), :])
+            down = link(here[t], cond[t, pl.ds(start + 1, height), :])
             diagonal = up + down + left[t] + right[t] + LEAKAGE * here[t] + jnp.where(here[t] > 0.0, 0.0, 1.0)
             most = jnp.maximum(diagonal, 1.0)
             root = lax.rsqrt(most)
@@ -285,21 +296,23 @@
             coef_c[t, at, :] = 2.0 * jnp.maximum(1.0 - diagonal, 0.0)
         return carry
 
-    lax.fori_loop(0, chunks + 2, links_chunk, 0)
+    sweep_border(links_rows)
+    sweep_own(links_rows)
 
     width_all = tiles * LANES * n_col
-    sub = lax.broadcasted_iota(jnp.int32, (8, LANES), 0)
-    columns = [my_col * (tiles * LANES) + t * LANES + lane for t in range(tiles)]
-    columns.append(my_col * (tiles * LANES) + jnp.where(lane < 64, tiles * LANES, -LANES) + lane)
-
-    def start_chunk(c, carry):
-        start = pl.multiple_of(8 + 8 * c, 8)
-        at, up_at, down_at = pl.ds(start, 8), pl.ds(start - 1, 8), pl.ds(start + 1, 8)
+
+    def start_rows(start, height, carry):
+        at, up_at, down_at = pl.ds(start, height), pl.ds(start - 1, height), pl.ds(start + 1, height)
+        column = lane_ids(height)
+        sub = lax.broadcasted_iota(jnp.int32, (height, LANES), 0)
+        first = my_col * (tiles * LANES)
+        columns = [first + t * LANES + column for t in range(tiles)]
+        columns.append(first + jnp.where(column < 64, tiles * LANES, -LANES) + column)
         root = [scale[t, at, :] for t in range(wide)]
         right = [link_e[t, at, :] for t in range(wide)]
         up = [link_n[t, at, :] for t in range(wide)]
         root_e = east(root)
-        flat = (my_row * rows + 8 * c - 8 + sub) * width_all
+        flat = (my_row * rows + start - OWN + sub) * width_all
         own = []
         for t in range(wide):
             coef_e[t, at, :] = 2.0 * right[t] * root[t] * root_e[t]
@@ -320,11 +333,11 @@
                 basis[0, p, t, at, :] = root[t] * (inject - total)
         return carry
 
-    lax.fori_loop(0, chunks + 2, start_chunk, 0)
-
-    def advance(k, c, sums):
-        start = pl.multiple_of(8 + 8 * c, 8)
-        at, up_at, down_at = pl.ds(start, 8), pl.ds(start - 1, 8), pl.ds(start + 1, 8)
+    sweep_border(start_rows)
+    sweep_own(start_rows)
+
+    def advance(k, start, height, sums):
+        at, up_at, down_at = pl.ds(start, height), pl.ds(start - 1, height), pl.ds(start + 1, height)
         final = k == STEPS - 1
         count = tiles if final else wide
         right = [coef_e[t, at, :] for t in range(wide)]
@@ -333,8 +346,8 @@
             here = [basis[k, p, t, at, :] for t in range(wide)]
             there = east(here)
             back = west([right[t] * here[t] for t in range(wide)])
-            same = jnp.zeros((8, LANES), jnp.float32)
-            step = jnp.zeros((8, LANES), jnp.float32)
+            same = jnp.zeros((height, LANES), jnp.float32)
+            step = jnp.zeros((height, LANES), jnp.float32)
             for t in range(count):
                 value = coef_c[t, at, :] * here[t] + right[t] * there[t] + back[t]
                 value = value + coef_n[t, at, :] * basis[k, p, t, up_at, :]
@@ -342,25 +355,27 @@
                 value = 0.5 * value if k < 2 else value - basis[k - 1, p, t, at, :]
                 if not final:
                     basis[k + 1, p, t, at, :] = value
-                if sums is not None and t < tiles:
+                if sums and t < tiles:
                     same = same + here[t] * here[t]
                     step = step + here[t] * value
-            if sums is not None:
+            if sums:
                 out += [sums[2 * p] + same, sums[2 * p + 1] + step]
-        return tuple(out)
+        return tuple(out) if sums else sums
+
+    def fold_rows(value):
+        total = value[:8]
+        for i in range(1, BLOCK // 8):
+            total = total + value[8 * i : 8 * i + 8]
+        return total
 
     for k in range(STEPS):
         if k < STEPS - 1:
-
-            def border(i, carry, k=k):
-                advance(k, i * (chunks + 1), None)
-                return carry
-
-            lax.fori_loop(0, 2, border, 0)
-        sums = lax.fori_loop(1, chunks + 1, functools.partial(advance, k), (zero,) * (2 * pairs))
+            sweep_border(functools.partial(advance, k))
+        tall_zero = jnp.zeros((BLOCK, LANES), jnp.float32)
+        sums = sweep_own(functools.partial(advance, k), (tall_zero,) * (2 * pairs))
         for p in range(pairs):
-            dots[(2 * k) * pairs + p] = sums[2 * p]
-            dots[(2 * k + 1) * pairs + p] = sums[2 * p + 1]
+            dots[(2 * k) * pairs + p] = fold_rows(sums[2 * p])
+            dots[(2 * k + 1) * pairs + p] = fold_rows(sums[2 * p + 1])
 
     n_dots = 2 * STEPS * pairs
     part = jnp.sum(dots[...], axis=1)
@@ -392,20 +407,21 @@
     message[...] = reduce_over("col", my_col, n_col, message, gather_col, 0)
     totals = reduce_over("row", my_row, n_row, message, gather_row, 1)
     parts = solve_coefficients([totals[j * pairs : (j + 1) * pairs] for j in range(2 * STEPS)])
-    weights = [[jnp.broadcast_to(part[p : p + 1], (8, LANES)) for part in parts] for p in range(pairs)]
-
-    def volts_chunk(c, carry):
-        at = pl.ds(pl.multiple_of(8 + 8 * c, 8), 8)
+    weights = [[jnp.broadcast_to(part[p : p + 1], (BLOCK, LANES)) for part in parts] for p in range(pairs)]
+
+    def volts_rows(start, height, carry):
+        at = pl.ds(start, height)
         for t in range(wide):
             root = scale[t, at, :]
             for p in range(pairs):
-                change = weights[p][0] * basis[0, p, t, at, :]
+                change = weights[p][0][:height] * basis[0, p, t, at, :]
                 for k in range(1, STEPS):
-                    change = change + weights[p][k] * basis[k, p, t, at, :]
+                    change = change + weights[p][k][:height] * basis[k, p, t, at, :]
                 volts[p, t, at, :] = volts[p, t, at, :] + root * change
         return carry
 
-    lax.fori_loop(0, chunks + 2, volts_chunk, 0)
+    sweep_border(volts_rows)
+    sweep_own(volts_rows)
     stores = []
     for t in range(tiles):
         for p in range(pairs):
@@ -421,9 +437,9 @@
 
     def currents(index):
         def body(i, carry):
-            row = index * quarter + 8 * i
+            row = index * quarter + BLOCK * i
             start = pl.multiple_of(OWN + row, 8)
-            at, up_at, down_at = pl.ds(start, 8), pl.ds(start - 1, 8), pl.ds(start + 1, 8)
+            at, up_at, down_at = pl.ds(start, BLOCK), pl.ds(start - 1, BLOCK), pl.ds(start + 1, BLOCK)
             right = [link_e[t, at, :] for t in range(wide)]
             total, peak = [None] * tiles, [None] * tiles
             for p in range(pairs):
@@ -438,13 +454,13 @@
                     value = 0.5 * value
                     total[t] = value if p == 0 else total[t] + value
                     peak[t] = value if p == 0 else jnp.maximum(peak[t], value)
-            to = pl.ds(pl.multiple_of(row, 8), 8)
+            to = pl.ds(pl.multiple_of(row, 8), BLOCK)
             for t in range(tiles):
                 local[0, to, pl.ds(t * LANES, LANES)] = total[t]
                 local[1, to, pl.ds(t * LANES, LANES)] = peak[t]
             return carry
 
-        lax.fori_loop(0, quarter // 8, body, 0)
+        lax.fori_loop(0, quarter // BLOCK, body, 0)
 
     q_next, q_prev = around(my_pair, 1, n_pair), around(my_pair, -1, n_pair)
     q_far = around(my_pair, 2, n_pair)
@@ -582,7 +598,7 @@
             pltpu.SemaphoreType.DMA((24,)),
         ],
         compiler_params=pltpu.CompilerParams(
-            collective_id=0, has_side_effects=True, vmem_limit_bytes=48 * 1024 * 1024
+            collective_id=0, has_side_effects=True, vmem_limit_bytes=60 * 1024 * 1024
         ),
     )(conductance, valid_mask, focal_cells, initial_volts)
 

time: 102 us -> 80.9 us (0.79)
  Pallas kernels: 94.9 us -> 75.7 us
  local copies, waits for them, and re-layouts: 6.54 us -> 4.35 us
    pallas_call x1, Pallas kernels: 94.9 us -> 75.7 us  [on_device(): pl.pallas_call(functools.partial(kernel, sizes), out_shape=(jax.ShapeDtyp...]
    unnamed x11 -> x7, local copies, waits for them, and re-layouts: 6.54 us -> 4.35 us
where the time goes in v2:
time: 80.9 us; the launch traced here: 80.7 us
  Pallas kernels  75.7 us (94%)
  local copies, waits for them, and re-layouts  4.35 us (5%)
    pallas_call x1, Pallas kernels, on_device(): pl.pallas_call(functools.partial(kernel, sizes), out_shape=(jax.ShapeDtyp...  75.7 us
    unnamed x7, local copies, waits for them, and re-layouts  4.35 us

profile of v2, /device:TPU:1, one launch (start us, length us, event | category | flops | bytes accessed | tf_op | source)
XLA Modules:
  0.0 80.7 jit_solution(6739757074618272999)
XLA Ops:
  0.6 75.7 %shard_map.67 = (f32[2,256,512]{2,1,0:T(8,128)}, f32[256,512]{1,0:T(8,128)}, f32[256,512]{1,0:T(8,128)}) custom-call(f32[256,512]{1,0:T(8,128)} %cond_in.1, s32[256,512]{1,0:T(8,128)} %mask_in.1, s32[2,2]{1,0:T(2,128)} %focal.1, f32[2,256,512]{2,1,0:T(8,128)} %volts_in.1), custom_call_target="tpu_custom_call" | custom-call | tf_op jit(solution)/shard_map/pallas_call | solution.py:557
  76.3 0.0 copy-start.1
  76.3 2.3 %copy.10 = f32[2,256,512]{2,1,0:T(8,128)} copy(f32[2,256,512]{2,1,0:T(8,128)} %get-tuple-element.6) | data formatting | bytes 2097152
  78.7 0.0 copy-done.1
  78.7 0.0 copy-start
  78.7 0.8 copy.11
  79.5 0.4 copy-done
  79.9 0.8 copy.12
Async XLA Ops:
  76.3 2.3 %copy-start.1 = (f32[256,512]{1,0:T(8,128)S(1)}, f32[256,512]{1,0:T(8,128)}, u32[]{:S(2)}) copy-start(f32[256,512]{1,0:T(8,128)} %get-tuple-element.7) | copy-start | bytes 1572868
  78.7 1.2 %copy-start = (f32[256,512]{1,0:T(8,128)S(1)}, f32[256,512]{1,0:T(8,128)}, u32[]{:S(2)}) copy-start(f32[256,512]{1,0:T(8,128)} %get-tuple-element.8) | copy-start | bytes 1572868

commit v3 on v2

--- a/solution.py
+++ b/solution.py
@@ -14,6 +14,7 @@
 EDGE = 8
 OWN = 16
 BLOCK = 32
+PIECES = 2
 
 
 def lane_ids(height):
@@ -83,8 +84,7 @@
     focal,
     volts_in,
     volts_out,
-    sum_out,
-    max_out,
+    result_out,
     stage_cond,
     stage_mask,
     volts,
@@ -105,16 +105,23 @@
     gather_col,
     gather_row,
     local,
-    far,
+    result,
     from_prev,
     from_next,
-    result,
+    far_volts,
+    far_basis,
+    cells,
+    far_cells,
+    shares,
+    far_shares,
     load_sem,
     store_sem,
     halo_send,
     halo_recv,
     red_send,
     red_recv,
+    far_send,
+    far_recv,
     ring_send,
     ring_recv,
 ):
@@ -146,11 +153,10 @@
 
     north, south = around(my_row, -1, n_row), around(my_row, 1, n_row)
     westward, eastward = around(my_col, -1, n_col), around(my_col, 1, n_col)
-    before, after = around(my_pair, -1, n_pair), around(my_pair, 1, n_pair)
     partners = [{"col": around(my_col, step, n_col)} for step in range(1, n_col)]
     partners += [{"row": around(my_row, step, n_row)} for step in range(1, n_row)]
     partners += [{"row": r, "col": c} for r in (north, south) for c in (westward, eastward)]
-    partners += [{"pair": before}, {"pair": after}]
+    partners += [{"pair": around(my_pair, step, n_pair)} for step in range(1, n_pair)]
     barrier = pltpu.get_barrier_semaphore()
     for partner in partners:
         pl.semaphore_signal(barrier, inc=1, device_id=partner, device_id_type=MESH)
@@ -165,6 +171,19 @@
                 volts[p, t, at, :] = zero
                 for k in range(STEPS):
                     basis[k, p, t, at, :] = zero
+    for start in (0, quarter + 3 * 8):
+        at = pl.ds(start, 8)
+        for p in range(pairs):
+            for t in range(wide):
+                far_volts[p, t, at, :] = zero
+                for k in range(STEPS):
+                    far_basis[k, p, t, at, :] = zero
+    row_of = lax.broadcasted_iota(jnp.int32, (8, LANES), 0)
+    packed_cells = jnp.zeros((8, LANES), jnp.int32)
+    for p in range(pairs):
+        for j in range(2):
+            packed_cells = jnp.where(row_of == 2 * p + j, focal[p, j], packed_cells)
+    cells[...] = packed_cells
 
     for load in loads:
         load.wait()
@@ -266,6 +285,31 @@
     unpack(pl.ds(0, 8), 3, over, has_n)
     unpack(pl.ds(fold + 8, 8), 0, under, has_s)
 
+    q_next, q_prev = around(my_pair, 1, n_pair), around(my_pair, -1, n_pair)
+    q_far = around(my_pair, 2, n_pair)
+
+    def to_far(slot, src, dst):
+        copy = pltpu.make_async_remote_copy(
+            src_ref=src,
+            dst_ref=dst,
+            send_sem=far_send.at[slot],
+            recv_sem=far_recv.at[slot],
+            device_id={"pair": q_far},
+            device_id_type=MESH,
+        )
+        copy.start()
+        return copy
+
+    far_rows = quarter + 2 * EDGE
+    far_copies = [
+        to_far(0, cells, far_cells),
+        to_far(
+            1,
+            volts.at[:, :, pl.ds(pl.multiple_of(OWN - EDGE + q_far * quarter, 8), far_rows)],
+            far_volts.at[:, :, pl.ds(8, far_rows)],
+        ),
+    ]
+
     def sweep_own(body, carry=()):
         def step(c, carry):
             return body(pl.multiple_of(OWN + BLOCK * c, 8), BLOCK, carry)
@@ -301,46 +345,59 @@
 
     width_all = tiles * LANES * n_col
 
-    def start_rows(start, height, carry):
+    def coefficient_rows(start, height, carry):
+        at = pl.ds(start, height)
+        root = [scale[t, at, :] for t in range(wide)]
+        root_e = east(root)
+        for t in range(wide):
+            coef_e[t, at, :] = 2.0 * link_e[t, at, :] * root[t] * root_e[t]
+            coef_n[t, at, :] = 2.0 * link_n[t, at, :] * root[t] * scale[t, pl.ds(start - 1, height), :]
+        return carry
+
+    def start_rows(field, out, ids, shift, start, height, carry):
         at, up_at, down_at = pl.ds(start, height), pl.ds(start - 1, height), pl.ds(start + 1, height)
+        base = pl.multiple_of(start + shift, 8)
+        own_at = pl.ds(base, height)
         column = lane_ids(height)
         sub = lax.broadcasted_iota(jnp.int32, (height, LANES), 0)
         first = my_col * (tiles * LANES)
         columns = [first + t * LANES + column for t in range(tiles)]
         columns.append(first + jnp.where(column < 64, tiles * LANES, -LANES) + column)
-        root = [scale[t, at, :] for t in range(wide)]
-        right = [link_e[t, at, :] for t in range(wide)]
-        up = [link_n[t, at, :] for t in range(wide)]
-        root_e = east(root)
-        flat = (my_row * rows + start - OWN + sub) * width_all
+        right = [link_e[t, own_at, :] for t in range(wide)]
+        flat = (my_row * rows + base - OWN + sub) * width_all
         own = []
         for t in range(wide):
-            coef_e[t, at, :] = 2.0 * right[t] * root[t] * root_e[t]
-            coef_n[t, at, :] = 2.0 * up[t] * root[t] * scale[t, up_at, :]
-            value = cond[t, at, :]
+            value = cond[t, own_at, :]
             own.append(LEAKAGE * value + jnp.where(value > 0.0, 0.0, 1.0))
         for p in range(pairs):
-            here = [volts[p, t, at, :] for t in range(wide)]
+            here = [field[p, t, at, :] for t in range(wide)]
             there = east(here)
             flow = [right[t] * (here[t] - there[t]) for t in range(wide)]
             flow_w = west(flow)
             for t in range(wide):
                 total = flow[t] - flow_w[t] + own[t] * here[t]
-                total = total + up[t] * (here[t] - volts[p, t, up_at, :])
-                total = total + link_n[t, down_at, :] * (here[t] - volts[p, t, down_at, :])
+                total = total + link_n[t, own_at, :] * (here[t] - field[p, t, up_at, :])
+                total = total + link_n[t, pl.ds(base + 1, height), :] * (here[t] - field[p, t, down_at, :])
                 cell = flat + columns[t]
-                inject = jnp.where(cell == focal[p, 0], 1.0, 0.0) - jnp.where(cell == focal[p, 1], 1.0, 0.0)
-                basis[0, p, t, at, :] = root[t] * (inject - total)
+                inject = jnp.where(cell == ids[2 * p], 1.0, 0.0) - jnp.where(cell == ids[2 * p + 1], 1.0, 0.0)
+                out[0, p, t, at, :] = scale[t, own_at, :] * (inject - total)
         return carry
 
-    sweep_border(start_rows)
-    sweep_own(start_rows)
-
-    def advance(k, start, height, sums):
+    sweep_border(coefficient_rows)
+    sweep_own(coefficient_rows)
+    start_own = functools.partial(
+        start_rows, volts, basis, [focal[p, j] for p in range(pairs) for j in range(2)], 0
+    )
+    sweep_border(start_own)
+    sweep_own(start_own)
+
+    def advance(basis, shift, k, start, height, sums):
         at, up_at, down_at = pl.ds(start, height), pl.ds(start - 1, height), pl.ds(start + 1, height)
+        base = pl.multiple_of(start + shift, 8)
+        own_at = pl.ds(base, height)
         final = k == STEPS - 1
         count = tiles if final else wide
-        right = [coef_e[t, at, :] for t in range(wide)]
+        right = [coef_e[t, own_at, :] for t in range(wide)]
         out = []
         for p in range(pairs):
             here = [basis[k, p, t, at, :] for t in range(wide)]
@@ -349,9 +406,9 @@
             same = jnp.zeros((height, LANES), jnp.float32)
             step = jnp.zeros((height, LANES), jnp.float32)
             for t in range(count):
-                value = coef_c[t, at, :] * here[t] + right[t] * there[t] + back[t]
-                value = value + coef_n[t, at, :] * basis[k, p, t, up_at, :]
-                value = value + coef_n[t, down_at, :] * basis[k, p, t, down_at, :]
+                value = coef_c[t, own_at, :] * here[t] + right[t] * there[t] + back[t]
+                value = value + coef_n[t, own_at, :] * basis[k, p, t, up_at, :]
+                value = value + coef_n[t, pl.ds(base + 1, height), :] * basis[k, p, t, down_at, :]
                 value = 0.5 * value if k < 2 else value - basis[k - 1, p, t, at, :]
                 if not final:
                     basis[k + 1, p, t, at, :] = value
@@ -370,9 +427,9 @@
 
     for k in range(STEPS):
         if k < STEPS - 1:
-            sweep_border(functools.partial(advance, k))
+            sweep_border(functools.partial(advance, basis, 0, k))
         tall_zero = jnp.zeros((BLOCK, LANES), jnp.float32)
-        sums = sweep_own(functools.partial(advance, k), (tall_zero,) * (2 * pairs))
+        sums = sweep_own(functools.partial(advance, basis, 0, k), (tall_zero,) * (2 * pairs))
         for p in range(pairs):
             dots[(2 * k) * pairs + p] = fold_rows(sums[2 * p])
             dots[(2 * k + 1) * pairs + p] = fold_rows(sums[2 * p + 1])
@@ -407,21 +464,24 @@
     message[...] = reduce_over("col", my_col, n_col, message, gather_col, 0)
     totals = reduce_over("row", my_row, n_row, message, gather_row, 1)
     parts = solve_coefficients([totals[j * pairs : (j + 1) * pairs] for j in range(2 * STEPS)])
-    weights = [[jnp.broadcast_to(part[p : p + 1], (BLOCK, LANES)) for part in parts] for p in range(pairs)]
-
-    def volts_rows(start, height, carry):
+    for k in range(STEPS):
+        shares[pl.ds(k * pairs, pairs), :] = parts[k]
+    far_copies.append(to_far(2, shares, far_shares))
+
+    def volts_rows(field, basis, shares, shift, start, height, carry):
         at = pl.ds(start, height)
-        for t in range(wide):
-            root = scale[t, at, :]
-            for p in range(pairs):
-                change = weights[p][0][:height] * basis[0, p, t, at, :]
+        for p in range(pairs):
+            for t in range(wide):
+                change = shares[pl.ds(p, 1), :] * basis[0, p, t, at, :]
                 for k in range(1, STEPS):
-                    change = change + weights[p][k][:height] * basis[k, p, t, at, :]
-                volts[p, t, at, :] = volts[p, t, at, :] + root * change
+                    change = change + shares[pl.ds(k * pairs + p, 1), :] * basis[k, p, t, at, :]
+                value = field[p, t, at, :] + scale[t, pl.ds(pl.multiple_of(start + shift, 8), height), :] * change
+                field[p, t, at, :] = value
         return carry
 
-    sweep_border(volts_rows)
-    sweep_own(volts_rows)
+    far_copies[1].wait_send()
+    sweep_border(functools.partial(volts_rows, volts, basis, shares, 0))
+    sweep_own(functools.partial(volts_rows, volts, basis, shares, 0))
     stores = []
     for t in range(tiles):
         for p in range(pairs):
@@ -432,38 +492,33 @@
                     store_sem.at[len(stores)],
                 )
             )
-    for store in stores:
-        store.start()
-
-    def currents(index):
-        def body(i, carry):
-            row = index * quarter + BLOCK * i
-            start = pl.multiple_of(OWN + row, 8)
-            at, up_at, down_at = pl.ds(start, BLOCK), pl.ds(start - 1, BLOCK), pl.ds(start + 1, BLOCK)
-            right = [link_e[t, at, :] for t in range(wide)]
-            total, peak = [None] * tiles, [None] * tiles
+
+
+    def currents(index, i, fields):
+        row = index * quarter + BLOCK * i
+        start = pl.multiple_of(OWN + row, 8)
+        right = [link_e[t, pl.ds(start, BLOCK), :] for t in range(wide)]
+        total, peak = [None] * tiles, [None] * tiles
+        for field, first in fields:
+            at, up_at, down_at = pl.ds(first, BLOCK), pl.ds(first - 1, BLOCK), pl.ds(first + 1, BLOCK)
             for p in range(pairs):
-                here = [volts[p, t, at, :] for t in range(wide)]
+                here = [field[p, t, at, :] for t in range(wide)]
                 there = east(here)
                 flow = [jnp.abs(right[t] * (here[t] - there[t])) for t in range(wide)]
                 flow_w = west(flow)
                 for t in range(tiles):
                     value = flow[t] + flow_w[t]
-                    value = value + jnp.abs(link_n[t, at, :] * (here[t] - volts[p, t, up_at, :]))
-                    value = value + jnp.abs(link_n[t, down_at, :] * (here[t] - volts[p, t, down_at, :]))
+                    value = value + jnp.abs(link_n[t, pl.ds(start, BLOCK), :] * (here[t] - field[p, t, up_at, :]))
+                    value = value + jnp.abs(
+                        link_n[t, pl.ds(start + 1, BLOCK), :] * (here[t] - field[p, t, down_at, :])
+                    )
                     value = 0.5 * value
-                    total[t] = value if p == 0 else total[t] + value
-                    peak[t] = value if p == 0 else jnp.maximum(peak[t], value)
-            to = pl.ds(pl.multiple_of(row, 8), BLOCK)
-            for t in range(tiles):
-                local[0, to, pl.ds(t * LANES, LANES)] = total[t]
-                local[1, to, pl.ds(t * LANES, LANES)] = peak[t]
-            return carry
-
-        lax.fori_loop(0, quarter // BLOCK, body, 0)
-
-    q_next, q_prev = around(my_pair, 1, n_pair), around(my_pair, -1, n_pair)
-    q_far = around(my_pair, 2, n_pair)
+                    total[t] = value if total[t] is None else total[t] + value
+                    peak[t] = value if peak[t] is None else jnp.maximum(peak[t], value)
+        to = pl.ds(pl.multiple_of(row, 8), BLOCK)
+        for t in range(tiles):
+            local[0, to, pl.ds(t * LANES, LANES)] = total[t]
+            local[1, to, pl.ds(t * LANES, LANES)] = peak[t]
 
     def span(index, u):
         return pl.ds(pl.multiple_of(index * quarter + u * unit, unit), unit)
@@ -481,29 +536,48 @@
         return copy
 
     in_unit = [pl.ds(u * unit, unit) for u in range(4)]
+    in_block = BLOCK // unit
     sent = {}
-    currents(q_far)
-    for i in range(2):
-        sent["far", i] = ring(i, local.at[:, span(q_far, i)], far.at[:, in_unit[i]], q_next)
-        sent["far", 2 + i] = ring(2 + i, local.at[:, span(q_far, 2 + i)], far.at[:, in_unit[2 + i]], q_prev)
-    currents(q_next)
-    for u in (2, 3):
-        sent["prev", u] = ring(4 + u, local.at[:, span(q_next, u)], from_prev.at[:, in_unit[u]], q_next)
-    currents(q_prev)
-    for u in (0, 1):
-        sent["next", u] = ring(8 + u, local.at[:, span(q_prev, u)], from_next.at[:, in_unit[u]], q_prev)
-    currents(my_pair)
-    for i in range(2):
-        for u, owner, name, base, target in (
-            (i, q_next, "prev", 4, from_prev),
-            (2 + i, q_prev, "next", 8, from_next),
-        ):
-            sent["far", u].wait_recv()
-            at = span(owner, u)
-            local[0, at, :] = local[0, at, :] + far[0, in_unit[u], :]
-            local[1, at, :] = jnp.maximum(local[1, at, :], far[1, in_unit[u], :])
-            sent[name, u] = ring(base + u, local.at[:, at], target.at[:, in_unit[u]], owner)
-    for u in (0, 2, 1, 3):
+    for i in range(quarter // BLOCK):
+        for owner, name, base, target in ((q_next, "prev", 0, from_prev), (q_prev, "next", 4, from_next)):
+            currents(owner, i, [(volts, pl.multiple_of(OWN + owner * quarter + BLOCK * i, 8))])
+            for u in range(i * in_block, (i + 1) * in_block):
+                sent[name, u] = ring(base + u, local.at[:, span(owner, u)], target.at[:, in_unit[u]], owner)
+
+    for store in stores:
+        store.start()
+
+    far_copies[0].wait_recv()
+    far_copies[1].wait_recv()
+    shift = my_pair * quarter
+    half = far_rows // 2
+
+    def sweep_far(body):
+        def step(c, carry):
+            return body(pl.multiple_of(8 + half * c, 8), half, carry)
+
+        lax.fori_loop(0, 2, step, ())
+
+    sweep_far(
+        functools.partial(
+            start_rows, far_volts, far_basis, [far_cells[pl.ds(r, 1), :] for r in range(2 * pairs)], shift
+        )
+    )
+    for k in range(STEPS - 1):
+        sweep_far(functools.partial(advance, far_basis, shift, k))
+    far_copies[2].wait_recv()
+    sweep_far(functools.partial(volts_rows, far_volts, far_basis, far_shares, shift))
+
+    for i in range(quarter // BLOCK):
+        currents(
+            my_pair,
+            i,
+            [
+                (volts, pl.multiple_of(OWN + my_pair * quarter + BLOCK * i, 8)),
+                (far_volts, OWN + BLOCK * i),
+            ],
+        )
+    for u in range(4):
         sent["prev", u].wait_recv()
         sent["next", u].wait_recv()
         at = span(my_pair, u)
@@ -511,34 +585,58 @@
         result[1, at, :] = jnp.maximum(
             local[1, at, :], jnp.maximum(from_prev[1, in_unit[u], :], from_next[1, in_unit[u], :])
         )
-        sent["up", u] = ring(12 + u, result.at[:, at], result.at[:, at], q_next)
-        sent["down", u] = ring(16 + u, result.at[:, at], result.at[:, at], q_prev)
+        sent["up", u] = ring(8 + u, result.at[:, at], result.at[:, at], q_next)
+        sent["down", u] = ring(12 + u, result.at[:, at], result.at[:, at], q_prev)
+
+    def keep(index, slot, first, count):
+        at = pl.ds(pl.multiple_of(index * quarter + first * unit, unit), count * unit)
+        stores.append(pltpu.make_async_copy(result.at[:, at], result_out.at[:, at], store_sem.at[pairs * tiles + slot]))
+        stores[-1].start()
+
     for i in range(2):
         sent["up", i].wait_recv()
         at = span(q_prev, i)
-        sent["over", i] = ring(20 + i, result.at[:, at], result.at[:, at], q_next)
+        sent["over", i] = ring(16 + i, result.at[:, at], result.at[:, at], q_next)
         sent["down", 2 + i].wait_recv()
         at = span(q_next, 2 + i)
-        sent["over", 2 + i] = ring(22 + i, result.at[:, at], result.at[:, at], q_prev)
+        sent["over", 2 + i] = ring(18 + i, result.at[:, at], result.at[:, at], q_prev)
+    keep(my_pair, 0, 0, 4)
     for i in range(2):
         sent["up", 2 + i].wait_recv()
         sent["down", i].wait_recv()
-
-    def keep(index, number):
-        at = pl.ds(pl.multiple_of(index * quarter, quarter), quarter)
-        base = pairs * tiles + 2 * number
-        for i, ref in enumerate((sum_out, max_out)):
-            stores.append(pltpu.make_async_copy(result.at[i, at], ref.at[at], store_sem.at[base + i]))
-            stores[-1].start()
-
-    keep(my_pair, 0)
-    keep(q_prev, 1)
-    keep(q_next, 2)
-    for u in range(4):
-        sent["over", u].wait_recv()
-    keep(q_far, 3)
+    keep(q_prev, 1, 0, 4)
+    keep(q_next, 2, 0, 4)
+    for i in range(2):
+        sent["over", i].wait_recv()
+        sent["over", 2 + i].wait_recv()
+        keep(q_far, 3 + 2 * i, i, 1)
+        keep(q_far, 4 + 2 * i, 2 + i, 1)
     for copy in sent.values():
         copy.wait_send()
+    far_copies[0].wait_send()
+    far_copies[2].wait_send()
+    for store in stores:
+        store.wait()
+
+
+def write_out(volts, result, volts_out, sum_out, max_out, held_volts, held_result, load_sem, store_sem):
+    pairs, rows = volts.shape[:2]
+    part = rows // PIECES
+    loads, stores = [], []
+    for i in range(PIECES):
+        at = pl.ds(i * part, part)
+        moves = [(volts.at[p, at], held_volts.at[p, at], volts_out.at[p, at]) for p in range(pairs)]
+        moves.append((result.at[0, at], held_result.at[0, at], sum_out.at[at]))
+        moves.append((result.at[1, at], held_result.at[1, at], max_out.at[at]))
+        for src, held, dst in moves:
+            n = len(loads)
+            loads.append(pltpu.make_async_copy(src, held, load_sem.at[n]))
+            stores.append(pltpu.make_async_copy(held, dst, store_sem.at[n]))
+    for load in loads:
+        load.start()
+    for load, store in zip(loads, stores):
+        load.wait()
+        store.start()
     for store in stores:
         store.wait()
 
@@ -552,28 +650,27 @@
     wide, tall, fold, quarter = tiles + 1, rows + 32, rows // 4, rows // 4
     n_dots = 2 * STEPS * pairs
     f32 = jnp.float32
-    anywhere = pl.BlockSpec(memory_space=pl.ANY)
-    field = pltpu.VMEM((wide, tall, LANES), f32)
-    return pl.pallas_call(
+    stay = pl.BlockSpec(memory_space=pltpu.HBM)
+    raster = pltpu.VMEM((wide, tall, LANES), f32)
+    volts, result = pl.pallas_call(
         functools.partial(kernel, sizes),
         out_shape=(
             jax.ShapeDtypeStruct((pairs, rows, columns), f32),
-            jax.ShapeDtypeStruct((rows, columns), f32),
-            jax.ShapeDtypeStruct((rows, columns), f32),
+            jax.ShapeDtypeStruct((2, rows, columns), f32),
         ),
-        in_specs=[anywhere, anywhere, pl.BlockSpec(memory_space=pltpu.SMEM), anywhere],
-        out_specs=(anywhere, anywhere, anywhere),
+        in_specs=[stay, stay, pl.BlockSpec(memory_space=pltpu.SMEM), stay],
+        out_specs=(stay, stay),
         scratch_shapes=[
             pltpu.VMEM((tiles, rows, LANES), f32),
             pltpu.VMEM((tiles, rows, LANES), jnp.int32),
             pltpu.VMEM((pairs, wide, tall, LANES), f32),
-            field,
-            field,
-            field,
-            field,
-            field,
-            field,
-            field,
+            raster,
+            raster,
+            raster,
+            raster,
+            raster,
+            raster,
+            raster,
             pltpu.VMEM((STEPS, pairs, wide, tall, LANES), f32),
             pltpu.VMEM((fold, LANES), f32),
             pltpu.VMEM((fold, LANES), f32),
@@ -584,23 +681,43 @@
             pltpu.VMEM((n_col, n_dots, LANES), f32),
             pltpu.VMEM((n_row, n_dots, LANES), f32),
             pltpu.VMEM((2, rows, columns), f32),
+            pltpu.VMEM((2, rows, columns), f32),
             pltpu.VMEM((2, quarter, columns), f32),
             pltpu.VMEM((2, quarter, columns), f32),
-            pltpu.VMEM((2, quarter, columns), f32),
-            pltpu.VMEM((2, rows, columns), f32),
+            pltpu.VMEM((pairs, wide, quarter + 32, LANES), f32),
+            pltpu.VMEM((STEPS, pairs, wide, quarter + 32, LANES), f32),
+            pltpu.VMEM((8, LANES), jnp.int32),
+            pltpu.VMEM((8, LANES), jnp.int32),
+            pltpu.VMEM((8 * ((STEPS * pairs + 7) // 8), LANES), f32),
+            pltpu.VMEM((8 * ((STEPS * pairs + 7) // 8), LANES), f32),
             pltpu.SemaphoreType.DMA(((2 + pairs) * tiles,)),
-            pltpu.SemaphoreType.DMA((pairs * tiles + 8,)),
+            pltpu.SemaphoreType.DMA((pairs * tiles + 7,)),
             pltpu.SemaphoreType.DMA((10,)),
             pltpu.SemaphoreType.DMA((10,)),
             pltpu.SemaphoreType.DMA((2, max(n_col, n_row) - 1)),
             pltpu.SemaphoreType.DMA((2, max(n_col, n_row) - 1)),
-            pltpu.SemaphoreType.DMA((24,)),
-            pltpu.SemaphoreType.DMA((24,)),
+            pltpu.SemaphoreType.DMA((3,)),
+            pltpu.SemaphoreType.DMA((3,)),
+            pltpu.SemaphoreType.DMA((20,)),
+            pltpu.SemaphoreType.DMA((20,)),
         ],
         compiler_params=pltpu.CompilerParams(
-            collective_id=0, has_side_effects=True, vmem_limit_bytes=60 * 1024 * 1024
+            collective_id=0, has_side_effects=True, vmem_limit_bytes=int(61 * 1024 * 1024)
         ),
     )(conductance, valid_mask, focal_cells, initial_volts)
+    flat = jax.ShapeDtypeStruct((rows, columns), f32)
+    return pl.pallas_call(
+        write_out,
+        out_shape=(jax.ShapeDtypeStruct((pairs, rows, columns), f32), flat, flat),
+        in_specs=[stay, stay],
+        out_specs=(stay, stay, stay),
+        scratch_shapes=[
+            pltpu.VMEM((pairs, rows, columns), f32),
+            pltpu.VMEM((2, rows, columns), f32),
+            pltpu.SemaphoreType.DMA((PIECES * (pairs + 2),)),
+            pltpu.SemaphoreType.DMA((PIECES * (pairs + 2),)),
+        ],
+    )(volts, result)
 
 
 def solution(mesh):

time: 80.9 us -> 74.4 us (0.920)
  local copies, waits for them, and re-layouts: 4.35 us -> 0 us
  Pallas kernels: 75.7 us -> 73.2 us
    pallas_call x1, Pallas kernels: 75.7 us -> 70.8 us  [on_device(): pl.pallas_call(functools.partial(kernel, sizes), out_shape=(jax.ShapeDtyp...]
    unnamed x7 -> x0, local copies, waits for them, and re-layouts: 4.35 us -> none
    pallas_call x0 -> x1, Pallas kernels: none -> 2.4 us  [on_device(): pl.pallas_call(write_out, out_shape=(jax.ShapeDtypeStruct((pairs, rows, c...]
where the time goes in v3:
time: 74.4 us; the launch traced here: 73.9 us
  Pallas kernels  73.2 us (98%)
    pallas_call x1, Pallas kernels, on_device(): pl.pallas_call(functools.partial(kernel, sizes), out_shape=(jax.ShapeDtyp...  70.8 us
    pallas_call x1, Pallas kernels, on_device(): pl.pallas_call(write_out, out_shape=(jax.ShapeDtypeStruct((pairs, rows, c...  2.4 us

profile of v3, /device:TPU:1, one launch (start us, length us, event | category | flops | bytes accessed | tf_op | source)
XLA Modules:
  0.0 73.9 jit_solution(12163449731011276177)
XLA Ops:
  0.6 70.8 %shard_map.67 = (f32[2,256,512]{2,1,0:T(8,128)}, f32[2,256,512]{2,1,0:T(8,128)}) custom-call(f32[256,512]{1,0:T(8,128)} %cond_in.1, s32[256,512]{1,0:T(8,128)} %mask_in.1, s32[2,2]{1,0:T(2,128)} %focal.1, f32[2,256,512]{2,1,0:T(8,128)} %volts_in.1), custom_call_target="tpu_custom_call" | custom-call | tf_op jit(solution)/shard_map/pallas_call | solution.py:655
  71.5 2.4 %shard_map.68 = (f32[2,256,512]{2,1,0:T(8,128)}, f32[256,512]{1,0:T(8,128)}, f32[256,512]{1,0:T(8,128)}) custom-call(f32[2,256,512]{2,1,0:T(8,128)} %get-tuple-element.5.volts, f32[2,256,512]{2,1,0:T(8,128)} %get-tuple-element.6.result), custom_call_target="tpu_custom_call" | custom-call | tf_op jit(solution)/shard_map/pallas_call | solution.py:709

commit v4 on v3

--- a/solution.py
+++ b/solution.py
@@ -14,6 +14,9 @@
 EDGE = 8
 OWN = 16
 BLOCK = 32
+SWEEP = 64
+HALF_BLOCK = 16
+NEAR_EARLY = 1
 PIECES = 2
 
 
@@ -104,12 +107,14 @@
     message,
     gather_col,
     gather_row,
-    local,
     result,
-    from_prev,
-    from_next,
+    late,
+    late_prev,
+    late_next,
     far_volts,
     far_basis,
+    far_pack,
+    land_pack,
     cells,
     far_cells,
     shares,
@@ -173,11 +178,12 @@
                     basis[k, p, t, at, :] = zero
     for start in (0, quarter + 3 * 8):
         at = pl.ds(start, 8)
-        for p in range(pairs):
-            for t in range(wide):
-                far_volts[p, t, at, :] = zero
-                for k in range(STEPS):
-                    far_basis[k, p, t, at, :] = zero
+        for s in range(n_pair - 1):
+            for p in range(pairs):
+                for t in range(wide):
+                    far_volts[s, p, t, at, :] = zero
+                    for k in range(STEPS):
+                        far_basis[s, k, p, t, at, :] = zero
     row_of = lax.broadcasted_iota(jnp.int32, (8, LANES), 0)
     packed_cells = jnp.zeros((8, LANES), jnp.int32)
     for p in range(pairs):
@@ -245,6 +251,52 @@
     ]
     for copy in halo:
         copy.start()
+
+    ahead = (1, n_pair - 1, 2)
+    owners = [around(my_pair, step, n_pair) for step in ahead]
+    early = (min(NEAR_EARLY, pairs), min(NEAR_EARLY, pairs), pairs)
+    moves = {}
+
+    def give(s, kind, src, dst):
+        slot = 5 * s + len([key for key in moves if key[0] == s])
+        moves[s, kind] = pltpu.make_async_remote_copy(
+            src_ref=src,
+            dst_ref=dst,
+            send_sem=far_send.at[slot],
+            recv_sem=far_recv.at[slot],
+            device_id={"pair": owners[s]},
+            device_id_type=MESH,
+        )
+        moves[s, kind].start()
+
+    def give_main(s):
+        if not early[s]:
+            return
+        start = pl.multiple_of(OWN + owners[s] * quarter, 8)
+        give(
+            s,
+            "main",
+            volts.at[pl.ds(0, early[s]), pl.ds(0, tiles), pl.ds(start, quarter)],
+            far_volts.at[s, pl.ds(0, early[s]), pl.ds(0, tiles), pl.ds(OWN, quarter)],
+        )
+
+    def give_border(s):
+        if not early[s]:
+            return
+        start = OWN + owners[s] * quarter
+        for kind, offset in (("over", -EDGE), ("under", quarter)):
+            give(
+                s,
+                kind,
+                volts.at[pl.ds(0, early[s]), pl.ds(0, tiles), pl.ds(pl.multiple_of(start + offset, 8), EDGE)],
+                far_volts.at[s, pl.ds(0, early[s]), pl.ds(0, tiles), pl.ds(OWN + offset, EDGE)],
+            )
+        give(s, "pack", far_pack.at[s], land_pack.at[s])
+        give(s, "cells", cells, far_cells.at[s])
+
+    give_main(0)
+    give_main(1)
+    give_main(2)
     for copy in halo:
         copy.wait()
 
@@ -285,36 +337,43 @@
     unpack(pl.ds(0, 8), 3, over, has_n)
     unpack(pl.ds(fold + 8, 8), 0, under, has_s)
 
-    q_next, q_prev = around(my_pair, 1, n_pair), around(my_pair, -1, n_pair)
-    q_far = around(my_pair, 2, n_pair)
-
-    def to_far(slot, src, dst):
-        copy = pltpu.make_async_remote_copy(
-            src_ref=src,
-            dst_ref=dst,
-            send_sem=far_send.at[slot],
-            recv_sem=far_recv.at[slot],
-            device_id={"pair": q_far},
-            device_id_type=MESH,
-        )
-        copy.start()
-        return copy
-
     far_rows = quarter + 2 * EDGE
-    far_copies = [
-        to_far(0, cells, far_cells),
-        to_far(
-            1,
-            volts.at[:, :, pl.ds(pl.multiple_of(OWN - EDGE + q_far * quarter, 8), far_rows)],
-            far_volts.at[:, :, pl.ds(8, far_rows)],
-        ),
-    ]
-
-    def sweep_own(body, carry=()):
+
+    def pack_place(j, p):
+        return 32 * (j % 4) + 16 * p
+
+    for s in range(n_pair - 1):
+        start = OWN - EDGE + owners[s] * quarter
+        for c in range(far_pack.shape[1] // 8):
+            packed = jnp.zeros((8, LANES), jnp.float32)
+            for j in range(4 * c, min(4 * c + 4, far_rows // 8)):
+                for p in range(early[s]):
+                    low = pack_place(j, p)
+                    value = volts[p, tiles, pl.ds(pl.multiple_of(start + 8 * j, 8), 8), :]
+                    moved = pltpu.roll(value, (low + 8) % LANES, 1)
+                    packed = jnp.where((lane >= low) & (lane < low + 16), moved, packed)
+            far_pack[s, pl.ds(8 * c, 8), :] = packed
+    give_border(0)
+    give_border(1)
+    give_border(2)
+
+    def take(s):
+        for kind in ("main", "over", "under", "pack", "cells"):
+            moves[s, kind].wait_recv()
+        for j in range(far_rows // 8):
+            for p in range(early[s]):
+                moved = pltpu.roll(
+                    land_pack[s, pl.ds(8 * (j // 4), 8), :], (2 * LANES - 8 - pack_place(j, p)) % LANES, 1
+                )
+                far_volts[s, p, tiles, pl.ds(8 + 8 * j, 8), :] = jnp.where(
+                    (lane < 8) | (lane >= LANES - 8), moved, 0.0
+                )
+
+    def sweep_own(body, carry=(), height=BLOCK):
         def step(c, carry):
-            return body(pl.multiple_of(OWN + BLOCK * c, 8), BLOCK, carry)
-
-        return lax.fori_loop(0, rows // BLOCK, step, carry)
+            return body(pl.multiple_of(OWN + height * c, 8), height, carry)
+
+        return lax.fori_loop(0, rows // height, step, carry)
 
     def sweep_border(body):
         def step(i, carry):
@@ -354,7 +413,7 @@
             coef_n[t, at, :] = 2.0 * link_n[t, at, :] * root[t] * scale[t, pl.ds(start - 1, height), :]
         return carry
 
-    def start_rows(field, out, ids, shift, start, height, carry):
+    def start_rows(count, field, out, ids, shift, start, height, carry):
         at, up_at, down_at = pl.ds(start, height), pl.ds(start - 1, height), pl.ds(start + 1, height)
         base = pl.multiple_of(start + shift, 8)
         own_at = pl.ds(base, height)
@@ -369,7 +428,7 @@
         for t in range(wide):
             value = cond[t, own_at, :]
             own.append(LEAKAGE * value + jnp.where(value > 0.0, 0.0, 1.0))
-        for p in range(pairs):
+        for p in range(count):
             here = [field[p, t, at, :] for t in range(wide)]
             there = east(here)
             flow = [right[t] * (here[t] - there[t]) for t in range(wide)]
@@ -386,12 +445,12 @@
     sweep_border(coefficient_rows)
     sweep_own(coefficient_rows)
     start_own = functools.partial(
-        start_rows, volts, basis, [focal[p, j] for p in range(pairs) for j in range(2)], 0
+        start_rows, pairs, volts, basis, [focal[p, j] for p in range(pairs) for j in range(2)], 0
     )
     sweep_border(start_own)
     sweep_own(start_own)
 
-    def advance(basis, shift, k, start, height, sums):
+    def advance(fields, basis, shift, k, start, height, sums):
         at, up_at, down_at = pl.ds(start, height), pl.ds(start - 1, height), pl.ds(start + 1, height)
         base = pl.multiple_of(start + shift, 8)
         own_at = pl.ds(base, height)
@@ -399,7 +458,7 @@
         count = tiles if final else wide
         right = [coef_e[t, own_at, :] for t in range(wide)]
         out = []
-        for p in range(pairs):
+        for p in range(fields):
             here = [basis[k, p, t, at, :] for t in range(wide)]
             there = east(here)
             back = west([right[t] * here[t] for t in range(wide)])
@@ -421,29 +480,47 @@
 
     def fold_rows(value):
         total = value[:8]
-        for i in range(1, BLOCK // 8):
+        for i in range(1, SWEEP // 8):
             total = total + value[8 * i : 8 * i + 8]
         return total
 
     for k in range(STEPS):
         if k < STEPS - 1:
-            sweep_border(functools.partial(advance, basis, 0, k))
-        tall_zero = jnp.zeros((BLOCK, LANES), jnp.float32)
-        sums = sweep_own(functools.partial(advance, basis, 0, k), (tall_zero,) * (2 * pairs))
+            sweep_border(functools.partial(advance, pairs, basis, 0, k))
+        tall_zero = jnp.zeros((SWEEP, LANES), jnp.float32)
+        sums = sweep_own(functools.partial(advance, pairs, basis, 0, k), (tall_zero,) * (2 * pairs), SWEEP)
         for p in range(pairs):
             dots[(2 * k) * pairs + p] = fold_rows(sums[2 * p])
             dots[(2 * k + 1) * pairs + p] = fold_rows(sums[2 * p + 1])
 
+    shift = my_pair * quarter
+    half = far_rows // 2
+
+    def sweep_far(body):
+        def step(c, carry):
+            return body(pl.multiple_of(8 + half * c, 8), half, carry)
+
+        lax.fori_loop(0, 2, step, ())
+
+    def far_pairs(s):
+        if not early[s]:
+            return
+        take(s)
+        ids = [far_cells[s, pl.ds(r, 1), :] for r in range(2 * pairs)]
+        sweep_far(functools.partial(start_rows, early[s], far_volts.at[s], far_basis.at[s], ids, shift))
+        for k in range(STEPS - 1):
+            sweep_far(functools.partial(advance, early[s], far_basis.at[s], shift, k))
+
     n_dots = 2 * STEPS * pairs
     part = jnp.sum(dots[...], axis=1)
     message[...] = jnp.broadcast_to(jnp.sum(part, axis=1, keepdims=True), (n_dots, LANES))
 
-    def reduce_over(axis, me, count, source, gather, phase):
+    def reduce_start(axis, me, count, gather, phase):
         copies = []
         for step in range(1, count):
             copies.append(
                 pltpu.make_async_remote_copy(
-                    src_ref=source,
+                    src_ref=message,
                     dst_ref=gather.at[me],
                     send_sem=red_send.at[phase, step - 1],
                     recv_sem=red_recv.at[phase, step - 1],
@@ -453,7 +530,10 @@
             )
         for copy in copies:
             copy.start()
-        gather[me] = source[...]
+        gather[me] = message[...]
+        return copies
+
+    def reduce_end(copies, count, gather):
         for copy in copies:
             copy.wait()
         total = gather[0]
@@ -461,16 +541,32 @@
             total = total + gather[i]
         return total
 
-    message[...] = reduce_over("col", my_col, n_col, message, gather_col, 0)
-    totals = reduce_over("row", my_row, n_row, message, gather_row, 1)
+    copies = reduce_start("col", my_col, n_col, gather_col, 0)
+    message[...] = reduce_end(copies, n_col, gather_col)
+    copies = reduce_start("row", my_row, n_row, gather_row, 1)
+    far_pairs(0)
+    totals = reduce_end(copies, n_row, gather_row)
     parts = solve_coefficients([totals[j * pairs : (j + 1) * pairs] for j in range(2 * STEPS)])
     for k in range(STEPS):
         shares[pl.ds(k * pairs, pairs), :] = parts[k]
-    far_copies.append(to_far(2, shares, far_shares))
-
-    def volts_rows(field, basis, shares, shift, start, height, carry):
+    tell = []
+    slots = [s for s in range(n_pair - 1) if early[s]]
+    for s in slots:
+        tell.append(
+            pltpu.make_async_remote_copy(
+                src_ref=shares,
+                dst_ref=far_shares.at[s],
+                send_sem=far_send.at[15 + s],
+                recv_sem=far_recv.at[15 + s],
+                device_id={"pair": owners[s]},
+                device_id_type=MESH,
+            )
+        )
+        tell[-1].start()
+
+    def volts_rows(count, field, basis, shares, shift, start, height, carry):
         at = pl.ds(start, height)
-        for p in range(pairs):
+        for p in range(count):
             for t in range(wide):
                 change = shares[pl.ds(p, 1), :] * basis[0, p, t, at, :]
                 for k in range(1, STEPS):
@@ -479,9 +575,10 @@
                 field[p, t, at, :] = value
         return carry
 
-    far_copies[1].wait_send()
-    sweep_border(functools.partial(volts_rows, volts, basis, shares, 0))
-    sweep_own(functools.partial(volts_rows, volts, basis, shares, 0))
+    for copy in moves.values():
+        copy.wait_send()
+    sweep_border(functools.partial(volts_rows, pairs, volts, basis, shares, 0))
+    sweep_own(functools.partial(volts_rows, pairs, volts, basis, shares, 0))
     stores = []
     for t in range(tiles):
         for p in range(pairs):
@@ -494,32 +591,28 @@
             )
 
 
-    def currents(index, i, fields):
-        row = index * quarter + BLOCK * i
+    def currents(row, height, fields, store):
         start = pl.multiple_of(OWN + row, 8)
-        right = [link_e[t, pl.ds(start, BLOCK), :] for t in range(wide)]
+        own_at = pl.ds(start, height)
+        right = [link_e[t, own_at, :] for t in range(wide)]
         total, peak = [None] * tiles, [None] * tiles
-        for field, first in fields:
-            at, up_at, down_at = pl.ds(first, BLOCK), pl.ds(first - 1, BLOCK), pl.ds(first + 1, BLOCK)
-            for p in range(pairs):
-                here = [field[p, t, at, :] for t in range(wide)]
-                there = east(here)
-                flow = [jnp.abs(right[t] * (here[t] - there[t])) for t in range(wide)]
-                flow_w = west(flow)
-                for t in range(tiles):
-                    value = flow[t] + flow_w[t]
-                    value = value + jnp.abs(link_n[t, pl.ds(start, BLOCK), :] * (here[t] - field[p, t, up_at, :]))
-                    value = value + jnp.abs(
-                        link_n[t, pl.ds(start + 1, BLOCK), :] * (here[t] - field[p, t, down_at, :])
-                    )
-                    value = 0.5 * value
-                    total[t] = value if total[t] is None else total[t] + value
-                    peak[t] = value if peak[t] is None else jnp.maximum(peak[t], value)
-        to = pl.ds(pl.multiple_of(row, 8), BLOCK)
+        for field, first, p in fields:
+            at, up_at, down_at = pl.ds(first, height), pl.ds(first - 1, height), pl.ds(first + 1, height)
+            here = [field[p, t, at, :] for t in range(wide)]
+            there = east(here)
+            flow = [jnp.abs(right[t] * (here[t] - there[t])) for t in range(wide)]
+            flow_w = west(flow)
+            for t in range(tiles):
+                value = flow[t] + flow_w[t]
+                value = value + jnp.abs(link_n[t, own_at, :] * (here[t] - field[p, t, up_at, :]))
+                value = value + jnp.abs(link_n[t, pl.ds(start + 1, height), :] * (here[t] - field[p, t, down_at, :]))
+                value = 0.5 * value
+                total[t] = value if total[t] is None else total[t] + value
+                peak[t] = value if peak[t] is None else jnp.maximum(peak[t], value)
         for t in range(tiles):
-            local[0, to, pl.ds(t * LANES, LANES)] = total[t]
-            local[1, to, pl.ds(t * LANES, LANES)] = peak[t]
-
+            store(pl.ds(t * LANES, LANES), total[t], peak[t])
+
+    q_next, q_prev, q_far = owners
     def span(index, u):
         return pl.ds(pl.multiple_of(index * quarter + u * unit, unit), unit)
 
@@ -535,58 +628,67 @@
         copy.start()
         return copy
 
-    in_unit = [pl.ds(u * unit, unit) for u in range(4)]
+    sent = {}
+
+    def spread(u, name):
+        at = span(my_pair, u)
+        if name == "up":
+            sent["up", u] = ring(u, result.at[:, at], result.at[:, at], q_next)
+        else:
+            sent["down", u] = ring(4 + u, result.at[:, at], result.at[:, at], q_prev)
+
+    arrays = late.shape[1]
+    near_pairs = range(early[0], pairs)
     in_block = BLOCK // unit
-    sent = {}
     for i in range(quarter // BLOCK):
-        for owner, name, base, target in ((q_next, "prev", 0, from_prev), (q_prev, "next", 4, from_next)):
-            currents(owner, i, [(volts, pl.multiple_of(OWN + owner * quarter + BLOCK * i, 8))])
+        for n, (owner, target) in enumerate(((q_next, late_prev), (q_prev, late_next))):
+            row = pl.multiple_of(owner * quarter + BLOCK * i, BLOCK)
+            at = pl.ds(BLOCK * i, BLOCK)
+
+            def store(lanes, total, peak, n=n, at=at):
+                late[n, 0, at, lanes] = total
+                if arrays > 1:
+                    late[n, 1, at, lanes] = peak
+
+            currents(row, BLOCK, [(volts, pl.multiple_of(OWN + row, 8), p) for p in near_pairs], store)
             for u in range(i * in_block, (i + 1) * in_block):
-                sent[name, u] = ring(base + u, local.at[:, span(owner, u)], target.at[:, in_unit[u]], owner)
-
+                part = pl.ds(u * unit, unit)
+                sent["late", n, u] = ring(12 + 2 * u + n, late.at[n, :, part], target.at[:, part], owner)
     for store in stores:
         store.start()
 
-    far_copies[0].wait_recv()
-    far_copies[1].wait_recv()
-    shift = my_pair * quarter
-    half = far_rows // 2
-
-    def sweep_far(body):
-        def step(c, carry):
-            return body(pl.multiple_of(8 + half * c, 8), half, carry)
-
-        lax.fori_loop(0, 2, step, ())
-
-    sweep_far(
-        functools.partial(
-            start_rows, far_volts, far_basis, [far_cells[pl.ds(r, 1), :] for r in range(2 * pairs)], shift
-        )
-    )
-    for k in range(STEPS - 1):
-        sweep_far(functools.partial(advance, far_basis, shift, k))
-    far_copies[2].wait_recv()
-    sweep_far(functools.partial(volts_rows, far_volts, far_basis, far_shares, shift))
-
+    far_pairs(1)
+    far_pairs(2)
+    for s, told in zip(slots, tell):
+        told.wait_recv()
+        sweep_far(functools.partial(volts_rows, early[s], far_volts.at[s], far_basis.at[s], far_shares.at[s], shift))
     for i in range(quarter // BLOCK):
-        currents(
-            my_pair,
-            i,
-            [
-                (volts, pl.multiple_of(OWN + my_pair * quarter + BLOCK * i, 8)),
-                (far_volts, OWN + BLOCK * i),
-            ],
-        )
-    for u in range(4):
-        sent["prev", u].wait_recv()
-        sent["next", u].wait_recv()
-        at = span(my_pair, u)
-        result[0, at, :] = local[0, at, :] + from_prev[0, in_unit[u], :] + from_next[0, in_unit[u], :]
-        result[1, at, :] = jnp.maximum(
-            local[1, at, :], jnp.maximum(from_prev[1, in_unit[u], :], from_next[1, in_unit[u], :])
-        )
-        sent["up", u] = ring(8 + u, result.at[:, at], result.at[:, at], q_next)
-        sent["down", u] = ring(12 + u, result.at[:, at], result.at[:, at], q_prev)
+
+        def own_block(h, carry, i=i):
+            at = BLOCK * i + HALF_BLOCK * h
+            row = pl.multiple_of(my_pair * quarter + at, HALF_BLOCK)
+            fields = [(volts, pl.multiple_of(OWN + row, 8), p) for p in range(pairs)]
+            for s in range(n_pair - 1):
+                fields += [(far_volts.at[s], pl.multiple_of(OWN + at, 8), p) for p in range(early[s])]
+
+            def store(lanes, total, peak):
+                result[0, pl.ds(row, HALF_BLOCK), lanes] = total
+                result[1, pl.ds(row, HALF_BLOCK), lanes] = peak
+
+            currents(row, HALF_BLOCK, fields, store)
+            return carry
+
+        lax.fori_loop(0, BLOCK // HALF_BLOCK, own_block, 0)
+        for u in range(i * in_block, (i + 1) * in_block):
+            at, rows_of = span(my_pair, u), pl.ds(u * unit, unit)
+            sent["late", 0, u].wait_recv()
+            sent["late", 1, u].wait_recv()
+            result[0, at, :] = result[0, at, :] + late_prev[0, rows_of, :] + late_next[0, rows_of, :]
+            result[1, at, :] = jnp.maximum(
+                result[1, at, :], jnp.maximum(late_prev[arrays - 1, rows_of, :], late_next[arrays - 1, rows_of, :])
+            )
+            spread(u, "up")
+            spread(u, "down")
 
     def keep(index, slot, first, count):
         at = pl.ds(pl.multiple_of(index * quarter + first * unit, unit), count * unit)
@@ -596,10 +698,10 @@
     for i in range(2):
         sent["up", i].wait_recv()
         at = span(q_prev, i)
-        sent["over", i] = ring(16 + i, result.at[:, at], result.at[:, at], q_next)
+        sent["over", i] = ring(8 + i, result.at[:, at], result.at[:, at], q_next)
         sent["down", 2 + i].wait_recv()
         at = span(q_next, 2 + i)
-        sent["over", 2 + i] = ring(18 + i, result.at[:, at], result.at[:, at], q_prev)
+        sent["over", 2 + i] = ring(10 + i, result.at[:, at], result.at[:, at], q_prev)
     keep(my_pair, 0, 0, 4)
     for i in range(2):
         sent["up", 2 + i].wait_recv()
@@ -613,8 +715,8 @@
         keep(q_far, 4 + 2 * i, 2 + i, 1)
     for copy in sent.values():
         copy.wait_send()
-    far_copies[0].wait_send()
-    far_copies[2].wait_send()
+    for copy in tell:
+        copy.wait_send()
     for store in stores:
         store.wait()
 
@@ -649,6 +751,9 @@
     sizes = (pairs, rows, tiles, n_pair, n_row, n_col)
     wide, tall, fold, quarter = tiles + 1, rows + 32, rows // 4, rows // 4
     n_dots = 2 * STEPS * pairs
+    others = n_pair - 1
+    arrays = min(2, pairs - NEAR_EARLY)
+    pack_rows = 8 * ((quarter // 8 + 2 + 3) // 4)
     f32 = jnp.float32
     stay = pl.BlockSpec(memory_space=pltpu.HBM)
     raster = pltpu.VMEM((wide, tall, LANES), f32)
@@ -681,23 +786,25 @@
             pltpu.VMEM((n_col, n_dots, LANES), f32),
             pltpu.VMEM((n_row, n_dots, LANES), f32),
             pltpu.VMEM((2, rows, columns), f32),
-            pltpu.VMEM((2, rows, columns), f32),
-            pltpu.VMEM((2, quarter, columns), f32),
-            pltpu.VMEM((2, quarter, columns), f32),
-            pltpu.VMEM((pairs, wide, quarter + 32, LANES), f32),
-            pltpu.VMEM((STEPS, pairs, wide, quarter + 32, LANES), f32),
+            pltpu.VMEM((2, arrays, quarter, columns), f32),
+            pltpu.VMEM((arrays, quarter, columns), f32),
+            pltpu.VMEM((arrays, quarter, columns), f32),
+            pltpu.VMEM((others, pairs, wide, quarter + 32, LANES), f32),
+            pltpu.VMEM((others, STEPS, pairs, wide, quarter + 32, LANES), f32),
+            pltpu.VMEM((others, pack_rows, LANES), f32),
+            pltpu.VMEM((others, pack_rows, LANES), f32),
             pltpu.VMEM((8, LANES), jnp.int32),
-            pltpu.VMEM((8, LANES), jnp.int32),
+            pltpu.VMEM((others, 8, LANES), jnp.int32),
             pltpu.VMEM((8 * ((STEPS * pairs + 7) // 8), LANES), f32),
-            pltpu.VMEM((8 * ((STEPS * pairs + 7) // 8), LANES), f32),
+            pltpu.VMEM((others, 8 * ((STEPS * pairs + 7) // 8), LANES), f32),
             pltpu.SemaphoreType.DMA(((2 + pairs) * tiles,)),
             pltpu.SemaphoreType.DMA((pairs * tiles + 7,)),
             pltpu.SemaphoreType.DMA((10,)),
             pltpu.SemaphoreType.DMA((10,)),
             pltpu.SemaphoreType.DMA((2, max(n_col, n_row) - 1)),
             pltpu.SemaphoreType.DMA((2, max(n_col, n_row) - 1)),
-            pltpu.SemaphoreType.DMA((3,)),
-            pltpu.SemaphoreType.DMA((3,)),
+            pltpu.SemaphoreType.DMA((18,)),
+            pltpu.SemaphoreType.DMA((18,)),
             pltpu.SemaphoreType.DMA((20,)),
             pltpu.SemaphoreType.DMA((20,)),
         ],

time: 74.4 us -> 71.8 us (0.965)
  Pallas kernels: 73.2 us -> 70 us
    pallas_call x1, Pallas kernels: 70.8 us -> 67.6 us  [on_device(): pl.pallas_call(functools.partial(kernel, sizes), out_shape=(jax.ShapeDtyp...]
where the time goes in v4:
time: 71.8 us; the launch traced here: 70.7 us
  Pallas kernels  70 us (97%)
    pallas_call x1, Pallas kernels, on_device(): pl.pallas_call(functools.partial(kernel, sizes), out_shape=(jax.ShapeDtyp...  67.6 us
    pallas_call x1, Pallas kernels, on_device(): pl.pallas_call(write_out, out_shape=(jax.ShapeDtypeStruct((pairs, rows, c...  2.4 us

profile of v4, /device:TPU:1, one launch (start us, length us, event | category | flops | bytes accessed | tf_op | source)
XLA Modules:
  0.0 70.7 jit_solution(1274511778264278613)
XLA Ops:
  0.6 67.6 %shard_map.67 = (f32[2,256,512]{2,1,0:T(8,128)}, f32[2,256,512]{2,1,0:T(8,128)}) custom-call(f32[256,512]{1,0:T(8,128)} %cond_in.1, s32[256,512]{1,0:T(8,128)} %mask_in.1, s32[2,2]{1,0:T(2,128)} %focal.1, f32[2,256,512]{2,1,0:T(8,128)} %volts_in.1), custom_call_target="tpu_custom_call" | custom-call | tf_op jit(solution)/shard_map/pallas_call | solution.py:760
  68.3 2.4 %shard_map.68 = (f32[2,256,512]{2,1,0:T(8,128)}, f32[256,512]{1,0:T(8,128)}, f32[256,512]{1,0:T(8,128)}) custom-call(f32[2,256,512]{2,1,0:T(8,128)} %get-tuple-element.5.volts, f32[2,256,512]{2,1,0:T(8,128)} %get-tuple-element.6.result), custom_call_target="tpu_custom_call" | custom-call | tf_op jit(solution)/shard_map/pallas_call | solution.py:816

commit v5 on v4

--- a/solution.py
+++ b/solution.py
@@ -369,7 +369,7 @@
                     (lane < 8) | (lane >= LANES - 8), moved, 0.0
                 )
 
-    def sweep_own(body, carry=(), height=BLOCK):
+    def sweep_own(body, carry=(), height=SWEEP):
         def step(c, carry):
             return body(pl.multiple_of(OWN + height * c, 8), height, carry)
 

time: 71.8 us -> 70.5 us (0.982)
  Pallas kernels: 70 us -> 69.1 us
    pallas_call x1, Pallas kernels: 67.6 us -> 66.7 us  [on_device(): pl.pallas_call(functools.partial(kernel, sizes), out_shape=(jax.ShapeDtyp...]
where the time goes in v5:
time: 70.5 us; the launch traced here: 69.7 us
  Pallas kernels  69.1 us (98%)
    pallas_call x1, Pallas kernels, on_device(): pl.pallas_call(functools.partial(kernel, sizes), out_shape=(jax.ShapeDtyp...  66.7 us
    pallas_call x1, Pallas kernels, on_device(): pl.pallas_call(write_out, out_shape=(jax.ShapeDtypeStruct((pairs, rows, c...  2.4 us

profile of v5, /device:TPU:1, one launch (start us, length us, event | category | flops | bytes accessed | tf_op | source)
XLA Modules:
  0.0 69.7 jit_solution(10751529512603533844)
XLA Ops:
  0.6 66.7 %shard_map.67 = (f32[2,256,512]{2,1,0:T(8,128)}, f32[2,256,512]{2,1,0:T(8,128)}) custom-call(f32[256,512]{1,0:T(8,128)} %cond_in.1, s32[256,512]{1,0:T(8,128)} %mask_in.1, s32[2,2]{1,0:T(2,128)} %focal.1, f32[2,256,512]{2,1,0:T(8,128)} %volts_in.1), custom_call_target="tpu_custom_call" | custom-call | tf_op jit(solution)/shard_map/pallas_call | solution.py:760
  67.3 2.4 %shard_map.68 = (f32[2,256,512]{2,1,0:T(8,128)}, f32[256,512]{1,0:T(8,128)}, f32[256,512]{1,0:T(8,128)}) custom-call(f32[2,256,512]{2,1,0:T(8,128)} %get-tuple-element.5.volts, f32[2,256,512]{2,1,0:T(8,128)} %get-tuple-element.6.result), custom_call_target="tpu_custom_call" | custom-call | tf_op jit(solution)/shard_map/pallas_call | solution.py:816

commit v6 on v5

--- a/solution.py
+++ b/solution.py
@@ -15,7 +15,7 @@
 OWN = 16
 BLOCK = 32
 SWEEP = 64
-HALF_BLOCK = 16
+HALF_BLOCK = 32
 NEAR_EARLY = 1
 PIECES = 2
 
@@ -564,9 +564,9 @@
         )
         tell[-1].start()
 
-    def volts_rows(count, field, basis, shares, shift, start, height, carry):
+    def volts_rows(which, field, basis, shares, shift, start, height, carry):
         at = pl.ds(start, height)
-        for p in range(count):
+        for p in which:
             for t in range(wide):
                 change = shares[pl.ds(p, 1), :] * basis[0, p, t, at, :]
                 for k in range(1, STEPS):
@@ -577,8 +577,8 @@
 
     for copy in moves.values():
         copy.wait_send()
-    sweep_border(functools.partial(volts_rows, pairs, volts, basis, shares, 0))
-    sweep_own(functools.partial(volts_rows, pairs, volts, basis, shares, 0))
+    sweep_border(functools.partial(volts_rows, range(early[0], pairs), volts, basis, shares, 0))
+    sweep_own(functools.partial(volts_rows, range(early[0], pairs), volts, basis, shares, 0))
     stores = []
     for t in range(tiles):
         for p in range(pairs):
@@ -654,6 +654,8 @@
             for u in range(i * in_block, (i + 1) * in_block):
                 part = pl.ds(u * unit, unit)
                 sent["late", n, u] = ring(12 + 2 * u + n, late.at[n, :, part], target.at[:, part], owner)
+    sweep_border(functools.partial(volts_rows, range(early[0]), volts, basis, shares, 0))
+    sweep_own(functools.partial(volts_rows, range(early[0]), volts, basis, shares, 0))
     for store in stores:
         store.start()
 
@@ -661,7 +663,7 @@
     far_pairs(2)
     for s, told in zip(slots, tell):
         told.wait_recv()
-        sweep_far(functools.partial(volts_rows, early[s], far_volts.at[s], far_basis.at[s], far_shares.at[s], shift))
+        sweep_far(functools.partial(volts_rows, range(early[s]), far_volts.at[s], far_basis.at[s], far_shares.at[s], shift))
     for i in range(quarter // BLOCK):
 
         def own_block(h, carry, i=i):

time: 70.5 us -> 70.3 us (level)
  no operation moved by 1% of the time
where the time goes in v6:
time: 70.3 us; the launch traced here: 69.2 us
  Pallas kernels  68.5 us (97%)
    pallas_call x1, Pallas kernels, on_device(): pl.pallas_call(functools.partial(kernel, sizes), out_shape=(jax.ShapeDtyp...  66.1 us
    pallas_call x1, Pallas kernels, on_device(): pl.pallas_call(write_out, out_shape=(jax.ShapeDtypeStruct((pairs, rows, c...  2.4 us

profile of v6, /device:TPU:1, one launch (start us, length us, event | category | flops | bytes accessed | tf_op | source)
XLA Modules:
  0.0 69.2 jit_solution(2578741470878332285)
XLA Ops:
  0.6 66.1 %shard_map.67 = (f32[2,256,512]{2,1,0:T(8,128)}, f32[2,256,512]{2,1,0:T(8,128)}) custom-call(f32[256,512]{1,0:T(8,128)} %cond_in.1, s32[256,512]{1,0:T(8,128)} %mask_in.1, s32[2,2]{1,0:T(2,128)} %focal.1, f32[2,256,512]{2,1,0:T(8,128)} %volts_in.1), custom_call_target="tpu_custom_call" | custom-call | tf_op jit(solution)/shard_map/pallas_call | solution.py:762
  66.8 2.4 %shard_map.68 = (f32[2,256,512]{2,1,0:T(8,128)}, f32[256,512]{1,0:T(8,128)}, f32[256,512]{1,0:T(8,128)}) custom-call(f32[2,256,512]{2,1,0:T(8,128)} %get-tuple-element.5.volts, f32[2,256,512]{2,1,0:T(8,128)} %get-tuple-element.6.result), custom_call_target="tpu_custom_call" | custom-call | tf_op jit(solution)/shard_map/pallas_call | solution.py:818
